TPU v7x, 256 devices: a whole 4x4x8 slice. The times are simulated.
256 devices in a mesh: tower: 2 (over z_hi), dp: 128 (over z_lo, x, y, core).
Axes of the slice: x: 4, y: 4, z: 8 (z_hi: 2, z_lo: 4; z = z_hi * 4 + z_lo), core: 2. Of those that a mesh axis runs over, the one named last changes fastest.
Arguments:
- picture_encoder_summary_vector: bfloat16 [8192, 1664], P('dp', 'tower'), may hold values from -6 to 6
- caption_encoder_summary_vector: bfloat16 [8192, 1280], P('dp', 'tower'), may hold values from -6 to 6
- picture_closing_norm_multiplier: float32 [1664], P('tower'), may hold values from 0.5 to 1.5
- caption_closing_norm_multiplier: float32 [1280], P('tower'), may hold values from 0.5 to 1.5
- picture_embedding_matrix: bfloat16 [1664, 1280], P('tower'), may hold values from -0.15625 to 0.15625
- caption_embedding_matrix: bfloat16 [1280, 1280], P('tower'), may hold values from -0.15625 to 0.15625
- similarity_sharpness: float32 [1], replicated, may hold values from 20 to 80
- similarity_offset: float32 [1], replicated, may hold values from -8 to -4
Outputs:
- image_proj_grad: float32 [1664, 1280], P('tower')
- text_proj_grad: float32 [1280, 1280], P('tower')
All inputs are finite; a program needn't handle non-finite values.
Results may differ from a plain program's by a relative error of at most 0.004.
Values may be sent and summed in bfloat16 or wider, within the bound.
No kernel may reach another device: no remote copies, remote signals or barrier semaphores. Data moves between devices by JAX's collectives and lax.ppermute only.
A program may use at most 128 MiB of HBM per device.

v0:
```python
import jax
import jax.numpy as jnp
from jax import lax
from jax.sharding import PartitionSpec as P


def partner(x, axis, stride):
    return lax.ppermute(x, axis, [(i, i ^ 1 << stride) for i in range(lax.axis_size(axis))])


def normed_half(values, sums, squares, width, gain):
    average = (sums / width)[:, None]
    inverse = lax.rsqrt((squares / width)[:, None] - average * average + 1e-06)
    return ((values - average) * inverse * gain[None, :]).astype(jnp.bfloat16)


def unit_rows(projected):
    length = jnp.sqrt(jnp.sum(projected * projected, axis=1, keepdims=True) + 1e-06)
    return (projected / length, length)


def pre_gradient(unit, length, gradient):
    along = jnp.sum(unit * gradient, axis=1, keepdims=True)
    return ((gradient - unit * along) / length).astype(jnp.bfloat16)


def pair_terms(own_rows, block_rows, own_first, column_ids, similarity_multiplier, bias_value):
    products = lax.dot_general(
        own_rows, block_rows, (((1,), (1,)), ((), ())), preferred_element_type=jnp.float32
    )
    logits = similarity_multiplier * products + bias_value
    row_ids = own_first + lax.broadcasted_iota(jnp.int32, products.shape, 0)
    labels = jnp.where(row_ids == column_ids[None, :], 1.0, -1.0).astype(jnp.float32)
    weights = (-labels * jax.nn.sigmoid(-labels * logits)).astype(jnp.bfloat16)
    return jnp.dot(weights, block_rows, preferred_element_type=jnp.float32)


def per_device(
    picture_encoder_summary_vector,
    caption_encoder_summary_vector,
    picture_closing_norm_multiplier,
    caption_closing_norm_multiplier,
    picture_embedding_matrix,
    caption_embedding_matrix,
    similarity_sharpness,
    similarity_offset,
):
    similarity_multiplier = similarity_sharpness[0]
    bias_value = similarity_offset[0]
    tower_count = lax.axis_size("tower")
    tower_index = lax.axis_index("tower")
    is_image = tower_index == 0
    row_count = picture_encoder_summary_vector.shape[0]
    own_first = lax.axis_index("dp") * row_count
    image_values = picture_encoder_summary_vector.astype(jnp.float32)
    text_values = caption_encoder_summary_vector.astype(jnp.float32)
    moments = lax.psum(
        (
            jnp.sum(image_values, axis=1),
            jnp.sum(image_values * image_values, axis=1),
            jnp.sum(text_values, axis=1),
            jnp.sum(text_values * text_values, axis=1),
        ),
        "tower",
    )
    image_normed = normed_half(
        image_values,
        moments[0],
        moments[1],
        picture_encoder_summary_vector.shape[1] * tower_count,
        picture_closing_norm_multiplier,
    )
    text_normed = normed_half(
        text_values,
        moments[2],
        moments[3],
        caption_encoder_summary_vector.shape[1] * tower_count,
        caption_closing_norm_multiplier,
    )
    projected = lax.psum(
        (
            jnp.dot(image_normed, picture_embedding_matrix, preferred_element_type=jnp.float32),
            jnp.dot(text_normed, caption_embedding_matrix, preferred_element_type=jnp.float32),
        ),
        "tower",
    )
    image_unit, image_length = unit_rows(projected[0])
    text_unit, text_length = unit_rows(projected[1])
    image_embed = image_unit.astype(jnp.bfloat16)
    text_embed = text_unit.astype(jnp.bfloat16)
    own_embed = jnp.where(is_image, image_embed, text_embed)
    other_embed = jnp.where(is_image, text_embed, image_embed)
    block_rows = lax.all_gather(other_embed, "dp", axis=0, tiled=True)
    column_ids = jnp.arange(block_rows.shape[0], dtype=jnp.int32)
    own_grad = similarity_multiplier * pair_terms(
        own_embed, block_rows, own_first, column_ids, similarity_multiplier, bias_value
    )
    partner_grad = partner(own_grad, "tower", 0)
    image_slope = pre_gradient(
        image_unit, image_length, jnp.where(is_image, own_grad, partner_grad)
    )
    text_slope = pre_gradient(text_unit, text_length, jnp.where(is_image, partner_grad, own_grad))
    image_term = lax.dot_general(
        image_normed, image_slope, (((0,), (0,)), ((), ())), preferred_element_type=jnp.float32
    )
    text_term = lax.dot_general(
        text_normed, text_slope, (((0,), (0,)), ((), ())), preferred_element_type=jnp.float32
    )
    weight_grads = lax.psum((image_term, text_term), "dp")
    return (weight_grads[0], weight_grads[1])


def solution(mesh):
    return jax.shard_map(
        per_device,
        mesh=mesh,
        in_specs=(
            P("dp", "tower"),
            P("dp", "tower"),
            P("tower"),
            P("tower"),
            P("tower", None),
            P("tower", None),
            P(),
            P(),
        ),
        out_specs=(P("tower", None), P("tower", None)),
        check_vma=False,
    )
```

profile of v0, /device:TPU:1, one launch (start us, length us, event | category | flops | bytes accessed | tf_op | source)
XLA Modules:
  0.0 1676.8 jit_solution(6166463563360325392)
XLA Ops:
  7.2 0.0 all-reduce.8.cloned.1.call-start
  7.2 1.2 convert_reduce_fusion
  8.4 1.0 convert_reduce_fusion.1
  9.4 10.1 all-reduce.1
  19.5 2.6 fusion.42
  22.1 1.2 fusion.45
  23.4 0.0 all-gather.2.cloned.1.call-start
  23.5 64.1 %all-reduce.8.cloned.1.call-done = (f32[64,1280]{1,0:T(8,128)}, f32[64,1280]{1,0:T(8,128)}) async-done(((f32[64,1280]{1,0:T(8,128)}, f32[64,1280]{1,0:T(8,128)}), (f32[64,1280]{1,0:T(8,128)}, f32[64,1280]{1,0:T(8,128)})) %all-reduce.8.cloned.1.call-update) | async-done | bytes 655376 | tf_op jit(solution)/shard_map/psum | solution.py:80
  87.5 1.1 multiply_reduce_fusion.3
  88.6 1.1 multiply_reduce_fusion.2
  89.8 1.9 broadcast_select_fusion.2
  91.6 0.0 all-gather.2.cloned.1.call-update
  91.7 0.0 all-reduce.6.cloned.1.call-start
  93.0 219.2 %all-gather.2.cloned.1.call-done = bf16[8192,1280]{1,0:T(8,128)(2,1)} async-done(((bf16[64,1280]{1,0:T(8,128)(2,1)}), bf16[8192,1280]{1,0:T(8,128)(2,1)}) %all-gather.2.cloned.1.call-update) | async-done | bytes 20971536 | tf_op jit(solution)/shard_map/all_gather | solution.py:93
  312.2 20.9 %fusion.9 = f32[64,1280]{1,0:T(8,128)S(1)} fusion(bf16[8192,1280]{1,0:T(8,128)(2,1)} %all-gather.2.cloned.1.call-done, f32[]{:T(128)} %bitcast.7, f32[]{:T(128)} %bitcast.6, s32[64]{0:T(128)S(1)} %iota_add_fusion, pred[]{:T(512)S(6)} %eq.11, f32[64,1280]{1,0:T(8,128)} %get-tuple-element.14, f32[64]{0:T(128)S(1)} %add_sqrt_fusion.1, ...), kind=kOutput, calls=%fused_computation.10 | convolution fusion | flops 2690613248 | bytes 21955336 | tf_op jit(solution)/shard_map/dot_general | solution.py:35
  333.1 3.6 collective-permute-start
  336.7 12.6 collective-permute-done
  349.3 0.3 multiply_reduce_fusion
  349.5 2.4 fusion.26
  352.0 2.9 fusion.25
  354.8 0.0 all-reduce.6.cloned.1.call-update
  354.9 1309.1 %all-reduce.6.cloned.1.call-done = (f32[832,1280]{1,0:T(8,128)}, f32[640,1280]{1,0:T(8,128)}) async-done(((f32[832,1280]{1,0:T(8,128)}, f32[640,1280]{1,0:T(8,128)}), (f32[832,1280]{1,0:T(8,128)}, f32[640,1280]{1,0:T(8,128)})) %all-reduce.6.cloned.1.call-update) | async-done | bytes 7536656 | tf_op jit(solution)/shard_map/psum | solution.py:109
  1663.9 4.7 copy.16
  1668.6 1.7 copy.17
  (21 shorter events, 0.1 us)
Async XLA Ops:
  7.2 15.0 copy-start
  7.2 15.0 copy-start.4
  7.2 15.0 copy-start.7
  7.2 80.3 %all-reduce.8.cloned.1.call-start = ((), (), s32[]{:S(2)}) async-start(), calls=%async_computation.2 | async-start | bytes 1310720 | tf_op jit(solution)/shard_map/psum | solution.py:80
  23.4 288.8 %all-gather.2.cloned.1.call-start = ((), (), s32[]{:S(2)}) async-start(), calls=%async_computation | async-start | bytes 21135360 | tf_op jit(solution)/shard_map/all_gather | solution.py:93
  91.7 1572.3 %all-reduce.6.cloned.1.call-start = ((), (), s32[]{:S(2)}) async-start(), calls=%async_computation.1 | async-start | bytes 15073280 | tf_op jit(solution)/shard_map/psum | solution.py:109
  312.2 37.1 %copy-start.1 = (f32[64,1280]{1,0:T(8,128)S(1)}, f32[64,1280]{1,0:T(8,128)}, u32[]{:S(2)}) copy-start(f32[64,1280]{1,0:T(8,128)} %get-tuple-element.14) | copy-start | bytes 983044
  312.2 37.1 %copy-start.2 = (f32[64,1280]{1,0:T(8,128)S(1)}, f32[64,1280]{1,0:T(8,128)}, u32[]{:S(2)}) copy-start(f32[64,1280]{1,0:T(8,128)} %get-tuple-element.15) | copy-start | bytes 983044
  312.2 37.3 %copy-start.5 = (bf16[64,640]{1,0:T(8,128)(2,1)S(1)}, bf16[64,640]{1,0:T(8,128)(2,1)}, u32[]{:S(2)}) copy-start(bf16[64,640]{1,0:T(8,128)(2,1)} %param.9) | copy-start | bytes 245764
  312.2 37.3 %copy-start.6 = (f32[640]{0:T(1024)S(1)}, f32[640]{0:T(1024)}, u32[]{:S(2)}) copy-start(f32[640]{0:T(1024)} %param.11) | copy-start | bytes 7684
  333.1 16.2 collective-permute-start
  1663.9 4.7 copy-start.3
Sparse Core Ops, SparseCore 0:
  23.5 63.9 all-reduce.7
  91.8 220.3 all-gather.1
  355.0 1308.8 all-reduce.5
where the time goes:
time: 1680 us
  waiting for transfers between devices  1600 us (95%)
  matrix products  30 us (2%)
    psum x1, waiting for transfers between devices, per_device(): weight_grads = lax.psum((image_term, text_term), 'dp')  1310 us
    all_gather x1, waiting for transfers between devices, per_device(): block_rows = lax.all_gather(other_embed, 'dp', axis=0, tiled=True)  219 us
    psum x1, waiting for transfers between devices, per_device(): lax.psum((jnp.dot(image_normed, picture_embedding_matrix, preferred_eleme...  64.1 us
  transfers between devices with their start and end apart: 4, of which 4 were waited for; matrix products, arithmetic and copies ran while one was open for 0% of the time, Pallas kernels for 0%

commit v1 on v0

v1 whole, which is shorter than its diff:
```python
import jax
import jax.numpy as jnp
from jax import lax
from jax.sharding import Mesh, PartitionSpec as P

AXES = ("t", "z", "x", "y", "c")
DP = ("z", "x", "y", "c")


def swap(x, axis, mask=1):
    return lax.ppermute(x, axis, [(i, i ^ mask) for i in range(lax.axis_size(axis))])


def normed_half(values, sums, squares, width, gain):
    average = (sums / width)[:, None]
    inverse = lax.rsqrt((squares / width)[:, None] - average * average + 1e-06)
    return ((values - average) * inverse * gain[None, :]).astype(jnp.bfloat16)


def split3(x):
    high = x.astype(jnp.bfloat16)
    rest = x - high.astype(jnp.float32)
    mid = rest.astype(jnp.bfloat16)
    low = (rest - mid.astype(jnp.float32)).astype(jnp.bfloat16)
    column = lax.broadcasted_iota(jnp.int32, (x.shape[0], 128), 1)
    zero = jnp.zeros((), jnp.bfloat16)
    return jnp.where(
        column == 0, high, jnp.where(column == 1, mid, jnp.where(column == 2, low, zero))
    )


def packed_rows(projected):
    length = jnp.sqrt(jnp.sum(projected * projected, axis=1, keepdims=True) + 1e-06)
    unit = (projected / length).astype(jnp.bfloat16)
    return jnp.concatenate([unit, split3(length)], axis=1)


def gather_xy(x):
    x = lax.all_gather(x, "y", axis=0, tiled=True)
    return lax.all_gather(x, "x", axis=0, tiled=True)


def gather_zc(x):
    x = lax.all_gather(x, "z", axis=0, tiled=True)
    other = swap(x, "c")
    first = lax.axis_index("c") == 0
    return jnp.concatenate([jnp.where(first, x, other), jnp.where(first, other, x)], axis=0)


def slope(gradient, packed, width):
    unit = packed[:, :width].astype(jnp.float32)
    length = jnp.sum(packed[:, width:].astype(jnp.float32), axis=1, keepdims=True)
    along = jnp.sum(unit * gradient, axis=1, keepdims=True)
    return ((gradient - unit * along) / length).astype(jnp.bfloat16)


def per_device(image_x, text_x, image_gain, text_gain, image_w, text_w, sharpness, offset):
    scale, bias = sharpness[0], offset[0]
    towers = lax.axis_size("t")
    rows, width = image_x.shape[0], image_w.shape[1]
    image_values = image_x.astype(jnp.float32)
    text_values = text_x.astype(jnp.float32)
    moments = lax.psum(
        (
            jnp.sum(image_values, axis=1),
            jnp.sum(image_values * image_values, axis=1),
            jnp.sum(text_values, axis=1),
            jnp.sum(text_values * text_values, axis=1),
        ),
        "t",
    )
    image_normed = normed_half(
        image_values, moments[0], moments[1], image_x.shape[1] * towers, image_gain
    )
    text_normed = normed_half(
        text_values, moments[2], moments[3], text_x.shape[1] * towers, text_gain
    )
    image_part = jnp.dot(image_normed, image_w, preferred_element_type=jnp.float32)
    text_part = jnp.dot(text_normed, text_w, preferred_element_type=jnp.float32)
    image_pre = image_part + swap(image_part.astype(jnp.bfloat16), "t").astype(jnp.float32)
    text_pre = text_part + swap(text_part.astype(jnp.bfloat16), "t").astype(jnp.float32)
    image_rows = gather_xy(packed_rows(image_pre))
    text_rows = gather_zc(packed_rows(text_pre))
    image_normed_rows = gather_xy(image_normed)
    text_normed_rows = gather_zc(text_normed)

    image_units, text_units = image_rows[:, :width], text_rows[:, :width]
    products = lax.dot_general(
        image_units, text_units, (((1,), (1,)), ((), ())), preferred_element_type=jnp.float32
    )
    logits = scale * products + bias
    sizes = {axis: lax.axis_size(axis) for axis in DP}
    own_image = (lax.axis_index("x") * sizes["y"] + lax.axis_index("y")) * rows
    own_text = (lax.axis_index("c") * sizes["z"] + lax.axis_index("z")) * rows
    row_ids = lax.broadcasted_iota(jnp.int32, products.shape, 0) - own_image
    column_ids = lax.broadcasted_iota(jnp.int32, products.shape, 1) - own_text
    same = (row_ids == column_ids) & (row_ids >= 0) & (row_ids < rows)
    labels = jnp.where(same, 1.0, -1.0).astype(jnp.float32)
    weights = (-labels * jax.nn.sigmoid(-labels * logits)).astype(jnp.bfloat16)
    image_grad = scale * jnp.dot(weights, text_units, preferred_element_type=jnp.float32)
    text_grad = scale * lax.dot_general(
        weights, image_units, (((0,), (0,)), ((), ())), preferred_element_type=jnp.float32
    )
    image_slope = slope(image_grad, image_rows, width)
    text_slope = slope(text_grad, text_rows, width)
    image_term = lax.dot_general(
        image_normed_rows, image_slope, (((0,), (0,)), ((), ())), preferred_element_type=jnp.float32
    )
    text_term = lax.dot_general(
        text_normed_rows, text_slope, (((0,), (0,)), ((), ())), preferred_element_type=jnp.float32
    )
    term = jnp.concatenate([image_term, text_term], axis=0)
    half = width // 2
    first = lax.axis_index("c") == 0
    kept = jnp.where(first, term[:, :half], term[:, half:])
    sent = jnp.where(first, term[:, half:], term[:, :half])
    kept = (kept + swap(sent, "c")).astype(jnp.bfloat16)
    groups = sizes["x"] * sizes["y"]
    blocks = kept.reshape(groups, kept.shape[0] // groups, half)
    blocks = lax.all_to_all(blocks, ("x", "y"), 0, 0)
    block = jnp.sum(blocks.astype(jnp.float32), axis=0).astype(jnp.bfloat16)
    others = [swap(block, "z", k).astype(jnp.float32) for k in range(1, sizes["z"])]
    block = (block.astype(jnp.float32) + others[0]) + (others[1] + others[2])
    block = block.astype(jnp.bfloat16)[None]
    block = gather_xy(block).reshape(kept.shape)
    other = swap(block, "c")
    full = jnp.concatenate(
        [jnp.where(first, block, other), jnp.where(first, other, block)], axis=1
    ).astype(jnp.float32)
    depth = image_w.shape[0]
    return full[:depth], full[depth:]


def solution(mesh):
    grid = Mesh(mesh.devices.reshape(2, 4, 4, 4, 2), AXES)
    return jax.shard_map(
        per_device,
        mesh=grid,
        in_specs=(
            P(DP, "t"),
            P(DP, "t"),
            P("t"),
            P("t"),
            P("t", None),
            P("t", None),
            P(),
            P(),
        ),
        out_specs=(P("t", None), P("t", None)),
        check_vma=False,
    )
```

time: 1680 us -> 262 us (0.16)
  waiting for transfers between devices: 1600 us -> 77.9 us
  blocking collectives: 10.1 us -> 106 us
    psum x2 -> x0, waiting for transfers between devices: 1370 us -> none  [the longest x1 1310 us: per_device(): weight_grads = lax.psum((image_term, text_term), 'dp')]
    all_gather x1 -> x3, waiting for transfers between devices: 219 us -> 49.8 us  [gather_xy(): return lax.all_gather(x, 'x', axis=0, tiled=True)]
    all_gather x0 -> x5, blocking collectives: none -> 65.3 us  [the longest x3 34.7 us: gather_xy(): x = lax.all_gather(x, 'y', axis=0, tiled=True)]
    all_to_all x0 -> x1, blocking collectives: none -> 30.6 us  [per_device(): blocks = lax.all_to_all(blocks, ('x', 'y'), 0, 0)]
  transfers between devices with their start and end apart: 4 -> 12, of which waited for: 4 -> 8; matrix products, arithmetic and copies ran while one was open for 0% -> 6% of each run, Pallas kernels for 0% -> 0%
where the time goes in v1:
time: 262 us
  blocking collectives  106 us (40%)
  waiting for transfers between devices  77.9 us (30%)
  matrix products  21.2 us (8%)
  starting transfers between devices  20.4 us (8%)
  between operations  15.3 us (6%)
  other arithmetic  12.7 us (5%)
  local copies, waits for them, and re-layouts  8.28 us (3%)
    all_gather x3, waiting for transfers between devices, gather_xy(): return lax.all_gather(x, 'x', axis=0, tiled=True)  49.8 us
    all_gather x3, blocking collectives, gather_xy(): x = lax.all_gather(x, 'y', axis=0, tiled=True)  34.7 us
    all_gather x2, blocking collectives, gather_zc(): x = lax.all_gather(x, 'z', axis=0, tiled=True)  30.6 us
    all_to_all x1, blocking collectives, per_device(): blocks = lax.all_to_all(blocks, ('x', 'y'), 0, 0)  30.6 us
    ppermute x9, waiting for transfers between devices, swap(): lax.ppermute(x, axis, [(i, i ^ mask) for i in range(lax.axis_size(axis))])  28.1 us
    ppermute x9, starting transfers between devices, swap(): lax.ppermute(x, axis, [(i, i ^ mask) for i in range(lax.axis_size(axis))])  20.1 us
    psum x1, blocking collectives, per_device(): lax.psum((jnp.sum(image_values, axis=1), jnp.sum(image_values * image_val...  10.1 us
    dot_general x1, matrix products, per_device(): lax.dot_general(image_normed_rows, image_slope, (((0,), (0,)), ((), ())),...  6.56 us
  transfers between devices with their start and end apart: 12, of which 8 were waited for; matrix products, arithmetic and copies ran while one was open for 6% of the time, Pallas kernels for 0%

profile of v1, /device:TPU:1, one launch (start us, length us, event | category | flops | bytes accessed | tf_op | source)
XLA Modules:
  0.0 261.7 jit_solution(13843849776653703867)
XLA Ops:
  9.4 10.1 %all-reduce = (f32[64]{0:T(128)S(1)}, f32[64]{0:T(128)S(1)}, f32[64]{0:T(128)S(1)}, f32[64]{0:T(128)S(1)}) all-reduce(f32[64]{0:T(128)S(1)} %get-tuple-element.5, f32[64]{0:T(128)S(1)} %get-tuple-element.4, f32[64]{0:T(128)S(1)} %get-tuple-element.3, f32[64]{0:T(128)S(1)} %get-tuple-element.2), channel_id=1, replica_groups=mesh['t'=2,'z'=4,'x'=4,'y'=4,'c'=2] {'t'}, use_global_device_ids=true, to_apply=%region_8.0 | all-reduce | flops 256 | bytes 2048 | tf_op jit(solution)/shard_map/psum | solution.py:63
  22.3 5.5 %collective-permute-start.1 = (bf16[64,1280]{1,0:T(8,128)(2,1)S(1)}, bf16[64,1280]{1,0:T(8,128)(2,1)S(1)}, u32[]{:S(2)}, u32[]{:S(2)}) collective-permute-start(bf16[64,1280]{1,0:T(8,128)(2,1)S(1)} %get-tuple-element.32), channel_id=1, source_target_pairs={{0,128},{128,0},{1,129},{129,1},{2,130},{130,2},{3,131},{131,3},{4... | collective-permute-start | bytes 491528 | tf_op jit(solution)/shard_map/ppermute | solution.py:11
  30.7 7.4 %collective-permute-done = bf16[64,1280]{1,0:T(8,128)(2,1)S(1)} collective-permute-done((bf16[64,1280]{1,0:T(8,128)(2,1)S(1)}, bf16[64,1280]{1,0:T(8,128)(2,1)S(1)}, u32[]{:S(2)}, u32[]{:S(2)}) %collective-permute-start) | collective-permute-done | bytes 163872 | tf_op jit(solution)/shard_map/ppermute | solution.py:11
  38.5 12.2 %all_gather.26 = bf16[256,1408]{1,0:T(8,128)(2,1)} all-gather(bf16[64,1408]{1,0:T(8,128)(2,1)S(1)} %pad_maximum_fusion.1), channel_id=1, replica_groups=mesh['t'=2,'z'=4,'x'=4,'y'=4,'c'=2] {'y'}, dimensions={0}, use_global_device_ids=true | all-gather | bytes 901120 | tf_op jit(solution)/shard_map/all_gather | solution.py:39
  50.8 15.2 %all_gather.29 = bf16[256,640]{1,0:T(8,128)(2,1)S(1)} all-gather(bf16[64,640]{1,0:T(8,128)(2,1)S(1)} %fusion.29), channel_id=1, replica_groups=mesh['t'=2,'z'=4,'x'=4,'y'=4,'c'=2] {'z'}, dimensions={0}, use_global_device_ids=true | all-gather | bytes 409600 | tf_op jit(solution)/shard_map/all_gather | solution.py:44
  65.9 7.5 %collective-permute-start.3 = (bf16[256,640]{1,0:T(8,128)(2,1)S(1)}, bf16[256,640]{1,0:T(8,128)(2,1)S(1)}, u32[]{:S(2)}, u32[]{:S(2)}) collective-permute-start(bf16[256,640]{1,0:T(8,128)(2,1)S(1)} %all_gather.29), channel_id=1, source_target_pairs={{0,1},{1,0},{2,3},{3,2},{4,5},{5,4},{6,7},{7,6},{8,9},{9,8},{10,11... | collective-permute-start | bytes 983048 | tf_op jit(solution)/shard_map/ppermute | solution.py:11
  73.6 15.4 %all_gather.28 = bf16[256,1408]{1,0:T(8,128)(2,1)S(1)} all-gather(bf16[64,1408]{1,0:T(8,128)(2,1)S(1)} %pad_maximum_fusion.2), channel_id=1, replica_groups=mesh['t'=2,'z'=4,'x'=4,'y'=4,'c'=2] {'z'}, dimensions={0}, use_global_device_ids=true | all-gather | bytes 901120 | tf_op jit(solution)/shard_map/all_gather | solution.py:44
  90.7 11.3 %all_gather.24 = bf16[256,832]{1,0:T(8,128)(2,1)} all-gather(bf16[64,832]{1,0:T(8,128)(2,1)S(1)} %fusion.25), channel_id=1, replica_groups=mesh['t'=2,'z'=4,'x'=4,'y'=4,'c'=2] {'y'}, dimensions={0}, use_global_device_ids=true | all-gather | bytes 532480 | tf_op jit(solution)/shard_map/all_gather | solution.py:39
  106.3 4.2 %multiply_convert_fusion = bf16[1024,512]{1,0:T(8,128)(2,1)S(1)} fusion(bf16[512,1280]{1,0:T(8,128)(2,1)S(1)} %fusion.15, bf16[1024,1408]{1,0:T(8,128)(2,1)} %all-gather.8.cloned.1.call-done, f32[]{:T(128)} %bitcast.17, f32[]{:T(128)} %bitcast.14, s32[512]{0:T(512)S(1)} %iota_subtract_fusion.1, s32[1024]{0:T(1024)S(1)} %iota_subtract_fusion, ...), kind=kOutput, calls=%fused_computation.20 | convolution fusion | flops 1348993024 | bytes 4989952 | tf_op jit(solution)/shard_map/dot_general | solution.py:88
  112.3 3.9 %fusion = (f32[1024]{0:T(1024)S(1)}, f32[1024,1280]{1,0:T(8,128)}) fusion(f32[]{:T(128)} %bitcast.13, bf16[1024,1408]{1,0:T(8,128)(2,1)S(1)} %copy-done.3, bf16[1024,512]{1,0:T(8,128)(2,1)S(1)} %multiply_convert_fusion, bf16[512,1280]{1,0:T(8,128)(2,1)S(1)} %fusion.15), kind=kOutput, calls=%fused_computation.4 | convolution fusion | flops 1347419136 | bytes 10227716 | tf_op jit(solution)/shard_map/dot_general | solution.py:100
  116.2 2.6 fusion.16
  118.8 16.3 %all-gather.6.cloned.1.call-done = bf16[1024,832]{1,0:T(8,128)(2,1)} async-done(((bf16[256,832]{1,0:T(8,128)(2,1)}), bf16[1024,832]{1,0:T(8,128)(2,1)}) %all-gather.6.cloned.1.call-update) | async-done | bytes 1703952 | tf_op jit(solution)/shard_map/all_gather | solution.py:40
  135.1 6.6 %fusion.9 = f32[832,1280]{1,0:T(8,128)S(1)} fusion(bf16[1024,832]{1,0:T(8,128)(2,1)} %all-gather.6.cloned.1.call-done, f32[1024,1280]{1,0:T(8,128)} %get-tuple-element.37, f32[1024]{0:T(1024)S(1)} %convert_reduce_fusion, f32[1024]{0:T(1024)S(1)} %get-tuple-element.36, f32[]{:T(128)} %bitcast.16, bf16[1024,1408]{1,0:T(8,128)(2,1)} %all-gather.8.cloned.1.call-done), kind=kOutput, calls=%fused_computation.19 | convolution fusion | flops 2188902400 | bytes 13967872 | tf_op jit(solution)/shard_map/dot_general | solution.py:106
  142.8 6.2 %collective-permute-done.4 = f32[1472,640]{1,0:T(8,128)S(1)} collective-permute-done((f32[1472,640]{1,0:T(8,128)S(1)}, f32[1472,640]{1,0:T(8,128)S(1)}, u32[]{:S(2)}, u32[]{:S(2)}) %collective-permute-start.4) | collective-permute-done | bytes 3768352 | tf_op jit(solution)/shard_map/ppermute | solution.py:11
  150.8 3.5 %reshape.80 = bf16[16,92,640]{2,1,0:T(8,128)(2,1)} reshape(bf16[1472,640]{1,0:T(8,128)(2,1)} %add_convert_fusion) | data formatting | bytes 3768320 | tf_op jit(solution)/shard_map/reshape | solution.py:119
  154.3 30.6 %all_to_all.5 = bf16[16,92,640]{2,1,0:T(8,128)(2,1)S(1)} all-to-all(bf16[16,92,640]{2,1,0:T(8,128)(2,1)} %reshape.80), channel_id=1, replica_groups=mesh['t'=2,'z'=4,'x'=4,'y'=4,'c'=2] {'x','y'}, dimensions={0} | all-to-all | bytes 3768320 | tf_op jit(solution)/shard_map/all_to_all | solution.py:120
  185.2 3.3 %collective-permute-start.7 = (bf16[92,640]{1,0:T(8,128)(2,1)S(1)}, bf16[92,640]{1,0:T(8,128)(2,1)S(1)}, u32[]{:S(2)}, u32[]{:S(2)}) collective-permute-start(bf16[92,640]{1,0:T(8,128)(2,1)S(1)} %reduce_sum.112), channel_id=1, source_target_pairs={{0,96},{32,64},{64,32},{96,0},{1,97},{33,65},{65,33},{97,1},{2,98}... | collective-permute-start | bytes 353288 | tf_op jit(solution)/shard_map/ppermute | solution.py:11
  188.9 2.0 collective-permute-done.7
  190.9 7.6 %collective-permute-done.6 = bf16[92,640]{1,0:T(8,128)(2,1)S(1)} collective-permute-done((bf16[92,640]{1,0:T(8,128)(2,1)S(1)}, bf16[92,640]{1,0:T(8,128)(2,1)S(1)}, u32[]{:S(2)}, u32[]{:S(2)}) %collective-permute-start.6) | collective-permute-done | bytes 117792 | tf_op jit(solution)/shard_map/ppermute | solution.py:11
  198.6 11.3 %all-gather.1 = bf16[4,92,640]{2,1,0:T(8,128)(2,1)} all-gather(bf16[1,92,640]{2,1,0:T(8,128)(2,1)S(1)} %fusion.31), channel_id=2, replica_groups=mesh['t'=2,'z'=4,'x'=4,'y'=4,'c'=2] {'y'}, dimensions={0}, use_global_device_ids=true | all-gather | bytes 588800 | tf_op jit(solution)/shard_map/all_gather | solution.py:39
  209.9 33.5 %all-gather.10.cloned.1.call-done = bf16[16,92,640]{2,1,0:T(8,128)(2,1)} async-done(((bf16[4,92,640]{2,1,0:T(8,128)(2,1)}), bf16[16,92,640]{2,1,0:T(8,128)(2,1)}) %all-gather.10.cloned.1.call-update) | async-done | bytes 1884176 | tf_op jit(solution)/shard_map/all_gather | solution.py:40
  243.4 2.4 reshape.81
  246.6 3.5 %collective-permute-done.8 = bf16[1472,640]{1,0:T(8,128)(2,1)S(1)} collective-permute-done((bf16[1472,640]{1,0:T(8,128)(2,1)S(1)}, bf16[1472,640]{1,0:T(8,128)(2,1)S(1)}, u32[]{:S(2)}, u32[]{:S(2)}) %collective-permute-start.8) | collective-permute-done | bytes 1884192 | tf_op jit(solution)/shard_map/ppermute | solution.py:11
  252.9 2.3 slice.42
  (65 shorter events, 22.3 us)
Async XLA Ops:
  7.2 21.4 %copy-start = (bf16[832,1280]{1,0:T(8,128)(2,1)S(1)}, bf16[832,1280]{1,0:T(8,128)(2,1)}, u32[]{:S(2)}) copy-start(bf16[832,1280]{1,0:T(8,128)(2,1)} %param.12) | copy-start | bytes 6389764
  7.2 20.6 %copy-start.4 = (bf16[64,832]{1,0:T(8,128)(2,1)S(1)}, bf16[64,832]{1,0:T(8,128)(2,1)}, u32[]{:S(2)}) copy-start(bf16[64,832]{1,0:T(8,128)(2,1)} %param.8) | copy-start | bytes 319492
  7.2 97.8 %all-gather.8.cloned.1.call-start = ((), (), s32[]{:S(2)}) async-start(), calls=%async_computation.2 | async-start | bytes 3604480 | tf_op jit(solution)/shard_map/all_gather | solution.py:40
  22.3 8.3 %collective-permute-start.1 = (bf16[64,1280]{1,0:T(8,128)(2,1)S(1)}, bf16[64,1280]{1,0:T(8,128)(2,1)S(1)}, u32[]{:S(2)}, u32[]{:S(2)}) collective-permute-start(bf16[64,1280]{1,0:T(8,128)(2,1)S(1)} %get-tuple-element.32), channel_id=1, source_target_pairs={{0,128},{128,0},{1,129},{129,1},{2,130},{130,2},{3,131},{131,3},{4... | collective-permute-start | bytes 491528 | tf_op jit(solution)/shard_map/ppermute | solution.py:11
  29.0 9.1 %collective-permute-start = (bf16[64,1280]{1,0:T(8,128)(2,1)S(1)}, bf16[64,1280]{1,0:T(8,128)(2,1)S(1)}, u32[]{:S(2)}, u32[]{:S(2)}) collective-permute-start(bf16[64,1280]{1,0:T(8,128)(2,1)S(1)} %get-tuple-element.30), channel_id=1, source_target_pairs={{0,128},{128,0},{1,129},{129,1},{2,130},{130,2},{3,131},{131,3},{4... | collective-permute-start | bytes 491528 | tf_op jit(solution)/shard_map/ppermute | solution.py:11
  50.7 84.4 %all-gather.6.cloned.1.call-start = ((), (), s32[]{:S(2)}) async-start(), calls=%async_computation.1 | async-start | bytes 2293760 | tf_op jit(solution)/shard_map/all_gather | solution.py:40
  65.9 37.7 %collective-permute-start.3 = (bf16[256,640]{1,0:T(8,128)(2,1)S(1)}, bf16[256,640]{1,0:T(8,128)(2,1)S(1)}, u32[]{:S(2)}, u32[]{:S(2)}) collective-permute-start(bf16[256,640]{1,0:T(8,128)(2,1)S(1)} %all_gather.29), channel_id=1, source_target_pairs={{0,1},{1,0},{2,3},{3,2},{4,5},{5,4},{6,7},{7,6},{8,9},{9,8},{10,11... | collective-permute-start | bytes 983048 | tf_op jit(solution)/shard_map/ppermute | solution.py:11
  89.0 15.6 %collective-permute-start.2 = (bf16[256,1408]{1,0:T(8,128)(2,1)S(1)}, bf16[256,1408]{1,0:T(8,128)(2,1)S(1)}, u32[]{:S(2)}, u32[]{:S(2)}) collective-permute-start(bf16[256,1408]{1,0:T(8,128)(2,1)S(1)} %all_gather.28), channel_id=1, source_target_pairs={{0,1},{1,0},{2,3},{3,2},{4,5},{5,4},{6,7},{7,6},{8,9},{9,8},{10,11... | collective-permute-start | bytes 2162696 | tf_op jit(solution)/shard_map/ppermute | solution.py:11
  102.1 141.3 %all-gather.10.cloned.1.call-start = ((), (), s32[]{:S(2)}) async-start(), calls=%async_computation.3 | async-start | bytes 2457600 | tf_op jit(solution)/shard_map/all_gather | solution.py:40
  104.8 7.4 %copy-start.2 = (bf16[512,1280]{1,0:T(8,128)(2,1)}, bf16[512,1280]{1,0:T(8,128)(2,1)S(1)}, u32[]{:S(2)}) copy-start(bf16[512,1280]{1,0:T(8,128)(2,1)S(1)} %fusion.15) | copy-start | bytes 3932164
  106.3 4.2 %copy-start.3 = (bf16[1024,1408]{1,0:T(8,128)(2,1)S(1)}, bf16[1024,1408]{1,0:T(8,128)(2,1)}, u32[]{:S(2)}) copy-start(bf16[1024,1408]{1,0:T(8,128)(2,1)} %all-gather.8.cloned.1.call-done) | copy-start | bytes 8650756
  112.2 3.9 %copy-start.5 = (bf16[256,640]{1,0:T(8,128)(2,1)S(1)}, bf16[256,640]{1,0:T(8,128)(2,1)}, u32[]{:S(2)}) copy-start(bf16[256,640]{1,0:T(8,128)(2,1)} %get-tuple-element.14) | copy-start | bytes 983044
  112.3 3.9 %copy-start.6 = (bf16[256,640]{1,0:T(8,128)(2,1)S(1)}, bf16[256,640]{1,0:T(8,128)(2,1)}, u32[]{:S(2)}) copy-start(bf16[256,640]{1,0:T(8,128)(2,1)} %get-tuple-element.15) | copy-start | bytes 983044
  142.0 6.9 %collective-permute-start.4 = (f32[1472,640]{1,0:T(8,128)S(1)}, f32[1472,640]{1,0:T(8,128)S(1)}, u32[]{:S(2)}, u32[]{:S(2)}) collective-permute-start(f32[1472,640]{1,0:T(8,128)S(1)} %broadcast_select_fusion.2), channel_id=1, source_target_pairs={{0,1},{1,0},{2,3},{3,2},{4,5},{5,4},{6,7},{7,6},{8,9},{9,8},{10,11... | collective-permute-start | bytes 11304968 | tf_op jit(solution)/shard_map/ppermute | solution.py:11
  185.2 5.7 %collective-permute-start.7 = (bf16[92,640]{1,0:T(8,128)(2,1)S(1)}, bf16[92,640]{1,0:T(8,128)(2,1)S(1)}, u32[]{:S(2)}, u32[]{:S(2)}) collective-permute-start(bf16[92,640]{1,0:T(8,128)(2,1)S(1)} %reduce_sum.112), channel_id=1, source_target_pairs={{0,96},{32,64},{64,32},{96,0},{1,97},{33,65},{65,33},{97,1},{2,98}... | collective-permute-start | bytes 353288 | tf_op jit(solution)/shard_map/ppermute | solution.py:11
  188.5 10.0 %collective-permute-start.6 = (bf16[92,640]{1,0:T(8,128)(2,1)S(1)}, bf16[92,640]{1,0:T(8,128)(2,1)S(1)}, u32[]{:S(2)}, u32[]{:S(2)}) collective-permute-start(bf16[92,640]{1,0:T(8,128)(2,1)S(1)} %reduce_sum.112), channel_id=1, source_target_pairs={{0,64},{32,96},{64,0},{96,32},{1,65},{33,97},{65,1},{97,33},{2,66}... | collective-permute-start | bytes 353288 | tf_op jit(solution)/shard_map/ppermute | solution.py:11
  188.5 10.0 %collective-permute-start.5 = (bf16[92,640]{1,0:T(8,128)(2,1)S(1)}, bf16[92,640]{1,0:T(8,128)(2,1)S(1)}, u32[]{:S(2)}, u32[]{:S(2)}) collective-permute-start(bf16[92,640]{1,0:T(8,128)(2,1)S(1)} %reduce_sum.112), channel_id=1, source_target_pairs={{0,32},{32,0},{64,96},{96,64},{1,33},{33,1},{65,97},{97,65},{2,34}... | collective-permute-start | bytes 353288 | tf_op jit(solution)/shard_map/ppermute | solution.py:11
  245.8 4.2 %collective-permute-start.8 = (bf16[1472,640]{1,0:T(8,128)(2,1)S(1)}, bf16[1472,640]{1,0:T(8,128)(2,1)S(1)}, u32[]{:S(2)}, u32[]{:S(2)}) collective-permute-start(bf16[1472,640]{1,0:T(8,128)(2,1)S(1)} %reshape.81), channel_id=1, source_target_pairs={{0,1},{1,0},{2,3},{3,2},{4,5},{5,4},{6,7},{7,6},{8,9},{9,8},{10,11... | collective-permute-start | bytes 5652488 | tf_op jit(solution)/shard_map/ppermute | solution.py:11
  252.4 2.9 %copy-start.1 = (bf16[832,1280]{1,0:T(8,128)(2,1)S(1)}, bf16[832,1280]{1,0:T(8,128)(2,1)}, u32[]{:S(2)}) copy-start(bf16[832,1280]{1,0:T(8,128)(2,1)} %param.12) | copy-start | bytes 6389764
Sparse Core Ops, SparseCore 0:
  50.8 47.5 all-gather.7
  102.2 32.8 all-gather.5
  210.0 33.3 all-gather.9

commit v2 on v1

--- a/solution.py
+++ b/solution.py
@@ -35,16 +35,59 @@
     return jnp.concatenate([unit, split3(length)], axis=1)
 
 
-def gather_xy(x):
-    x = lax.all_gather(x, "y", axis=0, tiled=True)
-    return lax.all_gather(x, "x", axis=0, tiled=True)
+def ordered(own, other, axis, mask, second, place):
+    index = lax.axis_index(axis)
+    if mask == 3:
+        first = index < 2
+    elif second:
+        first = (index == 0) | (index == 3)
+    else:
+        first = index % 2 == 0
+    lower, upper = jnp.where(first, own, other), jnp.where(first, other, own)
+    if second and mask == 1:
+        lower, upper = jnp.split(lower, 2, axis=place), jnp.split(upper, 2, axis=place)
+        pieces = [lower[0], upper[0], upper[1], lower[1]]
+    else:
+        pieces = [lower, upper]
+    return jnp.concatenate(pieces, axis=place)
+
+
+def gather_xy(block):
+    parts = [part[None, None] for part in jnp.split(block, 2, axis=0)]
+    for phase in range(2):
+        axes = ("x", "y") if phase == 0 else ("x", "x", "y", "y")
+        masks = ((1, 1), (3, 3)) if phase == 0 else ((1, 3, 1, 3), (3, 1, 3, 1))
+        if phase == 1:
+            parts = [half for part in parts[::-1] for half in jnp.split(part, 2, axis=2)]
+        for step in range(2):
+            others = [swap(p, a, m) for p, a, m in zip(parts, axes, masks[step])]
+            others = lax.optimization_barrier(others)
+            parts = [
+                ordered(p, o, a, m, step == 1, ("x", "y").index(a))
+                for p, o, a, m in zip(parts, others, axes, masks[step])
+            ]
+    parts = [part.reshape((-1,) + part.shape[2:]) for part in parts]
+    return jnp.concatenate(parts[2:] + parts[:2], axis=1)
+
+
+def by_core(x):
+    other = swap(x, "c")
+    first = lax.axis_index("c") == 0
+    return jnp.concatenate([jnp.where(first, x, other), jnp.where(first, other, x)], axis=0)
 
 
 def gather_zc(x):
-    x = lax.all_gather(x, "z", axis=0, tiled=True)
-    other = swap(x, "c")
-    first = lax.axis_index("c") == 0
-    return jnp.concatenate([jnp.where(first, x, other), jnp.where(first, other, x)], axis=0)
+    parts = [x] + [swap(x, "z", k) for k in range(1, lax.axis_size("z"))]
+    parts = [parts[0]] + list(lax.optimization_barrier(parts[1:]))
+    index = lax.axis_index("z")
+    even, low = index % 2 == 0, index < 2
+    pairs = [
+        [jnp.where(even, a, b), jnp.where(even, b, a)] for a, b in (parts[:2], parts[2:])
+    ]
+    parts = [jnp.where(low, a, b) for a, b in zip(*pairs)] + [
+        jnp.where(low, b, a) for a, b in zip(*pairs)
+    ]
+    return by_core(jnp.concatenate(parts, axis=0))
 
 
 def slope(gradient, packed, width):
@@ -79,10 +122,11 @@
     text_part = jnp.dot(text_normed, text_w, preferred_element_type=jnp.float32)
     image_pre = image_part + swap(image_part.astype(jnp.bfloat16), "t").astype(jnp.float32)
     text_pre = text_part + swap(text_part.astype(jnp.bfloat16), "t").astype(jnp.float32)
-    image_rows = gather_xy(packed_rows(image_pre))
-    text_rows = gather_zc(packed_rows(text_pre))
-    image_normed_rows = gather_xy(image_normed)
-    text_normed_rows = gather_zc(text_normed)
+    text_rows = gather_xy(packed_rows(text_pre)).reshape(-1, width + 128)
+    image_rows = gather_zc(packed_rows(image_pre))
+    text_normed_rows = lax.all_gather(text_normed, "y", axis=0, tiled=True)
+    text_normed_rows = lax.all_gather(text_normed_rows, "x", axis=0, tiled=True)
+    image_normed_rows = by_core(lax.all_gather(image_normed, "z", axis=0, tiled=True))
 
     image_units, text_units = image_rows[:, :width], text_rows[:, :width]
     products = lax.dot_general(
@@ -90,8 +134,8 @@
     )
     logits = scale * products + bias
     sizes = {axis: lax.axis_size(axis) for axis in DP}
-    own_image = (lax.axis_index("x") * sizes["y"] + lax.axis_index("y")) * rows
-    own_text = (lax.axis_index("c") * sizes["z"] + lax.axis_index("z")) * rows
+    own_image = (lax.axis_index("c") * sizes["z"] + lax.axis_index("z")) * rows
+    own_text = (lax.axis_index("x") * sizes["y"] + lax.axis_index("y")) * rows
     row_ids = lax.broadcasted_iota(jnp.int32, products.shape, 0) - own_image
     column_ids = lax.broadcasted_iota(jnp.int32, products.shape, 1) - own_text
     same = (row_ids == column_ids) & (row_ids >= 0) & (row_ids < rows)
@@ -115,14 +159,15 @@
     kept = jnp.where(first, term[:, :half], term[:, half:])
     sent = jnp.where(first, term[:, half:], term[:, :half])
     kept = (kept + swap(sent, "c")).astype(jnp.bfloat16)
-    groups = sizes["x"] * sizes["y"]
-    blocks = kept.reshape(groups, kept.shape[0] // groups, half)
-    blocks = lax.all_to_all(blocks, ("x", "y"), 0, 0)
+    deep = kept.shape[0]
+    chips = sizes["x"] * sizes["y"]
+    each = -(-deep // (chips * 32)) * 32
+    kept = jnp.pad(kept, ((0, chips * each - deep), (0, 0)))
+    blocks = lax.all_to_all(kept.reshape(chips, each, half), ("x", "y"), 0, 0)
     block = jnp.sum(blocks.astype(jnp.float32), axis=0).astype(jnp.bfloat16)
     others = [swap(block, "z", k).astype(jnp.float32) for k in range(1, sizes["z"])]
     block = (block.astype(jnp.float32) + others[0]) + (others[1] + others[2])
-    block = block.astype(jnp.bfloat16)[None]
-    block = gather_xy(block).reshape(kept.shape)
+    block = gather_xy(block.astype(jnp.bfloat16)).reshape(chips * each, half)[:deep]
     other = swap(block, "c")
     full = jnp.concatenate(
         [jnp.where(first, block, other), jnp.where(first, other, block)], axis=1

time: 262 us -> 246 us (0.939); the launches traced: 262 us -> 242 us
  starting transfers between devices: 20.4 us -> 66.5 us
  blocking collectives: 106 us -> 71 us
  waiting for transfers between devices: 77.9 us -> 54.4 us
  local copies, waits for them, and re-layouts: 8.28 us -> 2.79 us
    all_gather x3 -> x1, waiting for transfers between devices: 49.8 us -> 0.01 us  [per_device(): text_normed_rows = lax.all_gather(text_normed_rows, 'x', axis=0, tiled=True)]
    ppermute x9 -> x36, starting transfers between devices: 20.1 us -> 66.5 us  [swap(): lax.ppermute(x, axis, [(i, i ^ mask) for i in range(lax.axis_size(axis))])]
    all_gather x5 -> x2, blocking collectives: 65.3 us -> 29.3 us  [the longest x1 18 us: per_device(): lax.all_gather(image_normed, 'z', axis=0, tiled=True)]
    ppermute x9 -> x36, waiting for transfers between devices: 28.1 us -> 54.4 us  [swap(): lax.ppermute(x, axis, [(i, i ^ mask) for i in range(lax.axis_size(axis))])]
    reshape x2 -> x0, local copies, waits for them, and re-layouts: 5.93 us -> none  [the longest x1 3.52 us: per_device(): blocks = kept.reshape(groups, kept.shape[0] // groups, half)]
    dot_general x1, matrix products: 6.56 us -> 3.6 us  [per_device(): lax.dot_general(image_normed_rows, image_slope, (((0,), (0,)), ((), ())),...]
  transfers between devices with their start and end apart: 12 -> 37, of which waited for: 8 -> 21; matrix products, arithmetic and copies ran while one was open for 6% -> 7% of each run, Pallas kernels for 0% -> 0%
where the time goes in v2:
time: 246 us; the launch traced here: 242 us
  blocking collectives  71 us (29%)
  starting transfers between devices  66.5 us (27%)
  waiting for transfers between devices  54.4 us (22%)
  matrix products  19.1 us (8%)
  between operations  16.2 us (7%)
  other arithmetic  11.8 us (5%)
  local copies, waits for them, and re-layouts  2.79 us (1%)
    ppermute x36, starting transfers between devices, swap(): lax.ppermute(x, axis, [(i, i ^ mask) for i in range(lax.axis_size(axis))])  66.5 us
    ppermute x36, waiting for transfers between devices, swap(): lax.ppermute(x, axis, [(i, i ^ mask) for i in range(lax.axis_size(axis))])  54.4 us
    all_to_all x1, blocking collectives, per_device(): blocks = lax.all_to_all(kept.reshape(chips, each, half), ('x', 'y'), 0, 0)  31.7 us
    all_gather x1, blocking collectives, per_device(): lax.all_gather(image_normed, 'z', axis=0, tiled=True)  18 us
    all_gather x1, blocking collectives, per_device(): text_normed_rows = lax.all_gather(text_normed, 'y', axis=0, tiled=True)  11.3 us
    psum x1, blocking collectives, per_device(): lax.psum((jnp.sum(image_values, axis=1), jnp.sum(image_values * image_val...  10.1 us
    dot_general x1, matrix products, per_device(): lax.dot_general(text_normed_rows, text_slope, (((0,), (0,)), ((), ())), p...  5.22 us
  transfers between devices with their start and end apart: 37, of which 21 were waited for; matrix products, arithmetic and copies ran while one was open for 7% of the time, Pallas kernels for 0%

profile of v2, /device:TPU:1, one launch (start us, length us, event | category | flops | bytes accessed | tf_op | source)
XLA Modules:
  0.0 241.8 jit_solution(3573346572184453875)
XLA Ops:
  9.4 10.1 %all-reduce.1 = (f32[64]{0:T(128)S(1)}, f32[64]{0:T(128)S(1)}, f32[64]{0:T(128)S(1)}, f32[64]{0:T(128)S(1)}) all-reduce(f32[64]{0:T(128)S(1)} %get-tuple-element.59, f32[64]{0:T(128)S(1)} %get-tuple-element.58, f32[64]{0:T(128)S(1)} %get-tuple-element.57, ...), channel_id=1, replica_groups=mesh['t'=2,'z'=4,'x'=4,'y'=4,'c'=2] {'t'}, use_global_device_ids=true, to_apply=%region_8.0 | all-reduce | flops 256 | bytes 2048 | tf_op jit(solution)/shard_map/psum | solution.py:106
  20.5 11.3 %all_gather.10 = bf16[256,640]{1,0:T(8,128)(2,1)} all-gather(bf16[64,640]{1,0:T(8,128)(2,1)S(1)} %fusion.33), channel_id=1, replica_groups=mesh['t'=2,'z'=4,'x'=4,'y'=4,'c'=2] {'y'}, dimensions={0}, use_global_device_ids=true | all-gather | bytes 409600 | tf_op jit(solution)/shard_map/all_gather | solution.py:127
  33.6 4.9 %collective-permute-start.6 = (bf16[64,1280]{1,0:T(8,128)(2,1)S(1)}, bf16[64,1280]{1,0:T(8,128)(2,1)S(1)}, u32[]{:S(2)}, u32[]{:S(2)}) collective-permute-start(bf16[64,1280]{1,0:T(8,128)(2,1)S(1)} %get-tuple-element.158), channel_id=1, source_target_pairs={{0,128},{128,0},{1,129},{129,1},{2,130},{130,2},{3,131},{131,3},{4... | collective-permute-start | bytes 491528 | tf_op jit(solution)/shard_map/ppermute | solution.py:11
  42.1 7.0 %collective-permute-done.1 = bf16[64,1280]{1,0:T(8,128)(2,1)S(1)} collective-permute-done((bf16[64,1280]{1,0:T(8,128)(2,1)S(1)}, bf16[64,1280]{1,0:T(8,128)(2,1)S(1)}, u32[]{:S(2)}, u32[]{:S(2)}) %collective-permute-start.1) | collective-permute-done | bytes 163872 | tf_op jit(solution)/shard_map/ppermute | solution.py:11
  53.1 4.7 %collective-permute-start.2 = (bf16[64,1408]{1,0:T(8,128)(2,1)S(1)}, bf16[64,1408]{1,0:T(8,128)(2,1)S(1)}, u32[]{:S(2)}, u32[]{:S(2)}) collective-permute-start(bf16[64,1408]{1,0:T(8,128)(2,1)S(1)} %pad_maximum_fusion.22), channel_id=1, source_target_pairs={{0,32},{32,0},{64,96},{96,64},{1,33},{33,1},{65,97},{97,65},{2,34}... | collective-permute-start | bytes 540680 | tf_op jit(solution)/shard_map/ppermute | solution.py:11
  64.6 18.0 %all_gather.9 = bf16[256,832]{1,0:T(8,128)(2,1)S(1)} all-gather(bf16[64,832]{1,0:T(8,128)(2,1)S(1)} %fusion.27), channel_id=1, replica_groups=mesh['t'=2,'z'=4,'x'=4,'y'=4,'c'=2] {'z'}, dimensions={0}, use_global_device_ids=true | all-gather | bytes 532480 | tf_op jit(solution)/shard_map/all_gather | solution.py:129
  82.6 3.6 %collective-permute-start = (bf16[256,832]{1,0:T(8,128)(2,1)S(1)}, bf16[256,832]{1,0:T(8,128)(2,1)S(1)}, u32[]{:S(2)}, u32[]{:S(2)}) collective-permute-start(bf16[256,832]{1,0:T(8,128)(2,1)S(1)} %all_gather.9), channel_id=1, source_target_pairs={{0,1},{1,0},{2,3},{3,2},{4,5},{5,4},{6,7},{7,6},{8,9},{9,8},{10,11... | collective-permute-start | bytes 1277960 | tf_op jit(solution)/shard_map/ppermute | solution.py:11
  86.9 2.9 %collective-permute-start.12 = (bf16[1,4,16,1408]{3,2,1,0:T(8,128)(2,1)S(1)}, bf16[1,4,16,1408]{3,2,1,0:T(8,128)(2,1)S(1)}, u32[]{:S(2)}, u32[]{:S(2)}) collective-permute-start(bf16[1,4,16,1408]{3,2,1,0:T(8,128)(2,1)S(1)} %get-tuple-element.106), channel_id=1, source_target_pairs={{0,24},{8,16},{16,8},{24,0},{1,25},{9,17},{17,9},{25,1},{2,26},{10... | collective-permute-start | bytes 540680 | tf_op jit(solution)/shard_map/ppermute | solution.py:11
  89.9 2.4 collective-permute-start.13
  94.4 2.3 collective-permute-done.13
  100.3 2.7 %collective-permute-start.5 = (bf16[256,1408]{1,0:T(8,128)(2,1)S(1)}, bf16[256,1408]{1,0:T(8,128)(2,1)S(1)}, u32[]{:S(2)}, u32[]{:S(2)}) collective-permute-start(bf16[256,1408]{1,0:T(8,128)(2,1)S(1)} %pad_maximum_fusion.3), channel_id=1, source_target_pairs={{0,1},{1,0},{2,3},{3,2},{4,5},{5,4},{6,7},{7,6},{8,9},{9,8},{10,11... | collective-permute-start | bytes 2162696 | tf_op jit(solution)/shard_map/ppermute | solution.py:11
  103.1 5.1 %collective-permute-done.15 = bf16[2,4,16,1408]{3,2,1,0:T(8,128)(2,1)S(1)} collective-permute-done((bf16[2,4,16,1408]{3,2,1,0:T(8,128)(2,1)S(1)}, bf16[2,4,16,1408]{3,2,1,0:T(8,128)(2,1)S(1)}, u32[]{:S(2)}, u32[]{:S(2)}) %collective-permute-start.15) | collective-permute-done | bytes 360480 | tf_op jit(solution)/shard_map/ppermute | solution.py:11
  113.9 4.1 %fusion = (f32[1024]{0:T(1024)S(1)}, f32[1024,1280]{1,0:T(8,128)}) fusion(f32[]{:T(128)} %bitcast.40, bf16[1024,1408]{1,0:T(8,128)(2,1)S(1)} %bitcast.49, bf16[512,1024]{1,0:T(8,128)(2,1)S(1)} %multiply_convert_fusion, bf16[512,1280]{1,0:T(8,128)(2,1)S(1)} %fusion.15), kind=kOutput, calls=%fused_computation.4 | convolution fusion | flops 1347419136 | bytes 10227716 | tf_op jit(solution)/shard_map/dot_general | solution.py:145
  118.0 3.6 %fusion.16 = f32[832,1280]{1,0:T(8,128)} fusion(f32[512,1280]{1,0:T(8,128)S(1)} %get-tuple-element.165, bf16[512,1280]{1,0:T(8,128)(2,1)S(1)} %fusion.15, f32[512]{0:T(512)S(1)} %convert_reduce_fusion.2, f32[512]{0:T(512)S(1)} %get-tuple-element.164, bf16[256,832]{1,0:T(8,128)(2,1)S(1)} %get-tuple-element.69, bf16[256,832]{1,0:T(8,128)(2,1)S(1)} %get-tuple-element.68), kind=kOutput, calls=%fused_computation.34 | convolution fusion | flops 1095499776 | bytes 9048064 | tf_op jit(solution)/shard_map/dot_general | solution.py:150
  121.6 5.2 %fusion.9 = f32[640,1280]{1,0:T(8,128)S(1)} fusion(bf16[1024,640]{1,0:T(8,128)(2,1)} %all-gather.2.cloned.1.call-done, f32[1024,1280]{1,0:T(8,128)} %get-tuple-element.163, f32[1024]{0:T(1024)S(1)} %convert_reduce_fusion, f32[1024]{0:T(1024)S(1)} %get-tuple-element.162, f32[]{:T(128)} %bitcast.41, bf16[1024,1408]{1,0:T(8,128)(2,1)S(1)} %bitcast.50), kind=kOutput, calls=%fused_computation.20 | convolution fusion | flops 1685585920 | bytes 12460036 | tf_op jit(solution)/shard_map/dot_general | solution.py:153
  127.3 12.7 %collective-permute-start.19 = (f32[1472,640]{1,0:T(8,128)S(1)}, f32[1472,640]{1,0:T(8,128)S(1)}, u32[]{:S(2)}, u32[]{:S(2)}) collective-permute-start(f32[1472,640]{1,0:T(8,128)S(1)} %broadcast_select_fusion.2), channel_id=1, source_target_pairs={{0,1},{1,0},{2,3},{3,2},{4,5},{5,4},{6,7},{7,6},{8,9},{9,8},{10,11... | collective-permute-start | bytes 11304968 | tf_op jit(solution)/shard_map/ppermute | solution.py:11
  140.0 6.2 %collective-permute-done.19 = f32[1472,640]{1,0:T(8,128)S(1)} collective-permute-done((f32[1472,640]{1,0:T(8,128)S(1)}, f32[1472,640]{1,0:T(8,128)S(1)}, u32[]{:S(2)}, u32[]{:S(2)}) %collective-permute-start.19) | collective-permute-done | bytes 3768352 | tf_op jit(solution)/shard_map/ppermute | solution.py:11
  147.0 31.7 %all_to_all.5 = bf16[16,96,640]{2,1,0:T(8,128)(2,1)S(1)} all-to-all(bf16[16,96,640]{2,1,0:T(8,128)(2,1)S(1)} %bitcast.45), channel_id=1, replica_groups=mesh['t'=2,'z'=4,'x'=4,'y'=4,'c'=2] {'x','y'}, dimensions={0} | all-to-all | bytes 3932160 | tf_op jit(solution)/shard_map/all_to_all | solution.py:166
  184.7 6.8 %collective-permute-done.21 = bf16[96,640]{1,0:T(8,128)(2,1)S(1)} collective-permute-done((bf16[96,640]{1,0:T(8,128)(2,1)S(1)}, bf16[96,640]{1,0:T(8,128)(2,1)S(1)}, u32[]{:S(2)}, u32[]{:S(2)}) %collective-permute-start.21) | collective-permute-done | bytes 122912 | tf_op jit(solution)/shard_map/ppermute | solution.py:11
  192.2 2.6 %collective-permute-done.23 = bf16[1,1,48,640]{3,2,1,0:T(8,128)(2,1)S(1)} collective-permute-done((bf16[1,1,48,640]{3,2,1,0:T(8,128)(2,1)S(1)}, bf16[1,1,48,640]{3,2,1,0:T(8,128)(2,1)S(1)}, u32[]{:S(2)}, u32[]{:S(2)}) %collective-permute-start.23) | collective-permute-done | bytes 61472 | tf_op jit(solution)/shard_map/ppermute | solution.py:11
  211.7 3.6 %collective-permute-done.31 = bf16[2,4,24,640]{3,2,1,0:T(8,128)(2,1)S(1)} collective-permute-done((bf16[2,4,24,640]{3,2,1,0:T(8,128)(2,1)S(1)}, bf16[2,4,24,640]{3,2,1,0:T(8,128)(2,1)S(1)}, u32[]{:S(2)}, u32[]{:S(2)}) %collective-permute-start.31) | collective-permute-done | bytes 245792 | tf_op jit(solution)/shard_map/ppermute | solution.py:11
  218.1 8.0 %collective-permute-start.35 = (bf16[1472,640]{1,0:T(8,128)(2,1)S(1)}, bf16[1472,640]{1,0:T(8,128)(2,1)S(1)}, u32[]{:S(2)}, u32[]{:S(2)}) collective-permute-start(bf16[1472,640]{1,0:T(8,128)(2,1)S(1)} %slice.50), channel_id=1, source_target_pairs={{0,1},{1,0},{2,3},{3,2},{4,5},{5,4},{6,7},{7,6},{8,9},{9,8},{10,11... | collective-permute-start | bytes 5652488 | tf_op jit(solution)/shard_map/ppermute | solution.py:11
  226.1 3.5 %collective-permute-done.35 = bf16[1472,640]{1,0:T(8,128)(2,1)S(1)} collective-permute-done((bf16[1472,640]{1,0:T(8,128)(2,1)S(1)}, bf16[1472,640]{1,0:T(8,128)(2,1)S(1)}, u32[]{:S(2)}, u32[]{:S(2)}) %collective-permute-start.35) | collective-permute-done | bytes 1884192 | tf_op jit(solution)/shard_map/ppermute | solution.py:11
  232.4 2.3 slice.51
  (162 shorter events, 60.7 us)
Async XLA Ops:
  7.2 114.4 %all-gather.2.cloned.1.call-start = ((), (), s32[]{:S(2)}) async-start(), calls=%async_computation.1 | async-start | bytes 1638400 | tf_op jit(solution)/shard_map/all_gather | solution.py:128
  33.6 8.3 %collective-permute-start.6 = (bf16[64,1280]{1,0:T(8,128)(2,1)S(1)}, bf16[64,1280]{1,0:T(8,128)(2,1)S(1)}, u32[]{:S(2)}, u32[]{:S(2)}) collective-permute-start(bf16[64,1280]{1,0:T(8,128)(2,1)S(1)} %get-tuple-element.158), channel_id=1, source_target_pairs={{0,128},{128,0},{1,129},{129,1},{2,130},{130,2},{3,131},{131,3},{4... | collective-permute-start | bytes 491528 | tf_op jit(solution)/shard_map/ppermute | solution.py:11
  39.1 9.9 %collective-permute-start.1 = (bf16[64,1280]{1,0:T(8,128)(2,1)S(1)}, bf16[64,1280]{1,0:T(8,128)(2,1)S(1)}, u32[]{:S(2)}, u32[]{:S(2)}) collective-permute-start(bf16[64,1280]{1,0:T(8,128)(2,1)S(1)} %get-tuple-element.160), channel_id=1, source_target_pairs={{0,128},{128,0},{1,129},{129,1},{2,130},{130,2},{3,131},{131,3},{4... | collective-permute-start | bytes 491528 | tf_op jit(solution)/shard_map/ppermute | solution.py:11
  49.5 10.5 %collective-permute-start.7 = (bf16[1,1,32,1408]{3,2,1,0:T(8,128)(2,1)S(1)}, bf16[1,1,32,1408]{3,2,1,0:T(8,128)(2,1)S(1)}, u32[]{:S(2)}, u32[]{:S(2)}) collective-permute-start(bf16[1,1,32,1408]{3,2,1,0:T(8,128)(2,1)S(1)} %get-tuple-element.139), channel_id=1, source_target_pairs={{0,8},{8,0},{16,24},{24,16},{1,9},{9,1},{17,25},{25,17},{2,10},{10... | collective-permute-start | bytes 270344 | tf_op jit(solution)/shard_map/ppermute | solution.py:11
  50.8 9.2 %collective-permute-start.8 = (bf16[1,1,32,1408]{3,2,1,0:T(8,128)(2,1)S(1)}, bf16[1,1,32,1408]{3,2,1,0:T(8,128)(2,1)S(1)}, u32[]{:S(2)}, u32[]{:S(2)}) collective-permute-start(bf16[1,1,32,1408]{3,2,1,0:T(8,128)(2,1)S(1)} %get-tuple-element.138), channel_id=1, source_target_pairs={{0,2},{2,0},{4,6},{6,4},{1,3},{3,1},{5,7},{7,5},{8,10},{10,8},{12,... | collective-permute-start | bytes 270344 | tf_op jit(solution)/shard_map/ppermute | solution.py:11
  53.1 29.5 %collective-permute-start.2 = (bf16[64,1408]{1,0:T(8,128)(2,1)S(1)}, bf16[64,1408]{1,0:T(8,128)(2,1)S(1)}, u32[]{:S(2)}, u32[]{:S(2)}) collective-permute-start(bf16[64,1408]{1,0:T(8,128)(2,1)S(1)} %pad_maximum_fusion.22), channel_id=1, source_target_pairs={{0,32},{32,0},{64,96},{96,64},{1,33},{33,1},{65,97},{97,65},{2,34}... | collective-permute-start | bytes 540680 | tf_op jit(solution)/shard_map/ppermute | solution.py:11
  57.8 28.4 %collective-permute-start.3 = (bf16[64,1408]{1,0:T(8,128)(2,1)S(1)}, bf16[64,1408]{1,0:T(8,128)(2,1)S(1)}, u32[]{:S(2)}, u32[]{:S(2)}) collective-permute-start(bf16[64,1408]{1,0:T(8,128)(2,1)S(1)} %pad_maximum_fusion.22), channel_id=1, source_target_pairs={{0,64},{32,96},{64,0},{96,32},{1,65},{33,97},{65,1},{97,33},{2,66}... | collective-permute-start | bytes 540680 | tf_op jit(solution)/shard_map/ppermute | solution.py:11
  57.8 28.4 %collective-permute-start.4 = (bf16[64,1408]{1,0:T(8,128)(2,1)S(1)}, bf16[64,1408]{1,0:T(8,128)(2,1)S(1)}, u32[]{:S(2)}, u32[]{:S(2)}) collective-permute-start(bf16[64,1408]{1,0:T(8,128)(2,1)S(1)} %pad_maximum_fusion.22), channel_id=1, source_target_pairs={{0,96},{32,64},{64,32},{96,0},{1,97},{33,65},{65,33},{97,1},{2,98}... | collective-permute-start | bytes 540680 | tf_op jit(solution)/shard_map/ppermute | solution.py:11
  60.0 26.2 %collective-permute-start.9 = (bf16[2,1,32,1408]{3,2,1,0:T(8,128)(2,1)S(1)}, bf16[2,1,32,1408]{3,2,1,0:T(8,128)(2,1)S(1)}, u32[]{:S(2)}, u32[]{:S(2)}) collective-permute-start(bf16[2,1,32,1408]{3,2,1,0:T(8,128)(2,1)S(1)} %pad_maximum_fusion.23), channel_id=1, source_target_pairs={{0,24},{8,16},{16,8},{24,0},{1,25},{9,17},{17,9},{25,1},{2,26},{10... | collective-permute-start | bytes 540680 | tf_op jit(solution)/shard_map/ppermute | solution.py:11
  62.0 24.2 %collective-permute-start.10 = (bf16[1,2,32,1408]{3,2,1,0:T(8,128)(2,1)S(1)}, bf16[1,2,32,1408]{3,2,1,0:T(8,128)(2,1)S(1)}, u32[]{:S(2)}, u32[]{:S(2)}) collective-permute-start(bf16[1,2,32,1408]{3,2,1,0:T(8,128)(2,1)S(1)} %pad_maximum_fusion.24), channel_id=1, source_target_pairs={{0,6},{2,4},{4,2},{6,0},{1,7},{3,5},{5,3},{7,1},{8,14},{10,12},{12... | collective-permute-start | bytes 540680 | tf_op jit(solution)/shard_map/ppermute | solution.py:11
  82.6 17.7 %collective-permute-start = (bf16[256,832]{1,0:T(8,128)(2,1)S(1)}, bf16[256,832]{1,0:T(8,128)(2,1)S(1)}, u32[]{:S(2)}, u32[]{:S(2)}) collective-permute-start(bf16[256,832]{1,0:T(8,128)(2,1)S(1)} %all_gather.9), channel_id=1, source_target_pairs={{0,1},{1,0},{2,3},{3,2},{4,5},{5,4},{6,7},{7,6},{8,9},{9,8},{10,11... | collective-permute-start | bytes 1277960 | tf_op jit(solution)/shard_map/ppermute | solution.py:11
  86.3 6.5 %collective-permute-start.11 = (bf16[1,4,16,1408]{3,2,1,0:T(8,128)(2,1)S(1)}, bf16[1,4,16,1408]{3,2,1,0:T(8,128)(2,1)S(1)}, u32[]{:S(2)}, u32[]{:S(2)}) collective-permute-start(bf16[1,4,16,1408]{3,2,1,0:T(8,128)(2,1)S(1)} %get-tuple-element.107), channel_id=1, source_target_pairs={{0,8},{8,0},{16,24},{24,16},{1,9},{9,1},{17,25},{25,17},{2,10},{10... | collective-permute-start | bytes 540680 | tf_op jit(solution)/shard_map/ppermute | solution.py:11
  86.9 7.4 %collective-permute-start.12 = (bf16[1,4,16,1408]{3,2,1,0:T(8,128)(2,1)S(1)}, bf16[1,4,16,1408]{3,2,1,0:T(8,128)(2,1)S(1)}, u32[]{:S(2)}, u32[]{:S(2)}) collective-permute-start(bf16[1,4,16,1408]{3,2,1,0:T(8,128)(2,1)S(1)} %get-tuple-element.106), channel_id=1, source_target_pairs={{0,24},{8,16},{16,8},{24,0},{1,25},{9,17},{17,9},{25,1},{2,26},{10... | collective-permute-start | bytes 540680 | tf_op jit(solution)/shard_map/ppermute | solution.py:11
  89.9 6.8 %collective-permute-start.13 = (bf16[4,1,16,1408]{3,2,1,0:T(8,128)(2,1)S(1)}, bf16[4,1,16,1408]{3,2,1,0:T(8,128)(2,1)S(1)}, u32[]{:S(2)}, u32[]{:S(2)}) collective-permute-start(bf16[4,1,16,1408]{3,2,1,0:T(8,128)(2,1)S(1)} %get-tuple-element.103), channel_id=1, source_target_pairs={{0,2},{2,0},{4,6},{6,4},{1,3},{3,1},{5,7},{7,5},{8,10},{10,8},{12,... | collective-permute-start | bytes 540680 | tf_op jit(solution)/shard_map/ppermute | solution.py:11
  98.7 9.4 %collective-permute-start.15 = (bf16[2,4,16,1408]{3,2,1,0:T(8,128)(2,1)S(1)}, bf16[2,4,16,1408]{3,2,1,0:T(8,128)(2,1)S(1)}, u32[]{:S(2)}, u32[]{:S(2)}) collective-permute-start(bf16[2,4,16,1408]{3,2,1,0:T(8,128)(2,1)S(1)} %pad_maximum_fusion.13), channel_id=1, source_target_pairs={{0,24},{8,16},{16,8},{24,0},{1,25},{9,17},{17,9},{25,1},{2,26},{10... | collective-permute-start | bytes 1081352 | tf_op jit(solution)/shard_map/ppermute | solution.py:11
  99.2 9.0 %collective-permute-start.16 = (bf16[2,4,16,1408]{3,2,1,0:T(8,128)(2,1)S(1)}, bf16[2,4,16,1408]{3,2,1,0:T(8,128)(2,1)S(1)}, u32[]{:S(2)}, u32[]{:S(2)}) collective-permute-start(bf16[2,4,16,1408]{3,2,1,0:T(8,128)(2,1)S(1)} %pad_maximum_fusion.14), channel_id=1, source_target_pairs={{0,8},{8,0},{16,24},{24,16},{1,9},{9,1},{17,25},{25,17},{2,10},{10... | collective-permute-start | bytes 1081352 | tf_op jit(solution)/shard_map/ppermute | solution.py:11
  99.4 8.9 %collective-permute-start.17 = (bf16[4,2,16,1408]{3,2,1,0:T(8,128)(2,1)S(1)}, bf16[4,2,16,1408]{3,2,1,0:T(8,128)(2,1)S(1)}, u32[]{:S(2)}, u32[]{:S(2)}) collective-permute-start(bf16[4,2,16,1408]{3,2,1,0:T(8,128)(2,1)S(1)} %pad_maximum_fusion.12), channel_id=1, source_target_pairs={{0,6},{2,4},{4,2},{6,0},{1,7},{3,5},{5,3},{7,1},{8,14},{10,12},{12... | collective-permute-start | bytes 1081352 | tf_op jit(solution)/shard_map/ppermute | solution.py:11
  99.9 8.4 %collective-permute-start.18 = (bf16[4,2,16,1408]{3,2,1,0:T(8,128)(2,1)S(1)}, bf16[4,2,16,1408]{3,2,1,0:T(8,128)(2,1)S(1)}, u32[]{:S(2)}, u32[]{:S(2)}) collective-permute-start(bf16[4,2,16,1408]{3,2,1,0:T(8,128)(2,1)S(1)} %pad_maximum_fusion.15), channel_id=1, source_target_pairs={{0,2},{2,0},{4,6},{6,4},{1,3},{3,1},{5,7},{7,5},{8,10},{10,8},{12,... | collective-permute-start | bytes 1081352 | tf_op jit(solution)/shard_map/ppermute | solution.py:11
  100.3 9.2 %collective-permute-start.5 = (bf16[256,1408]{1,0:T(8,128)(2,1)S(1)}, bf16[256,1408]{1,0:T(8,128)(2,1)S(1)}, u32[]{:S(2)}, u32[]{:S(2)}) collective-permute-start(bf16[256,1408]{1,0:T(8,128)(2,1)S(1)} %pad_maximum_fusion.3), channel_id=1, source_target_pairs={{0,1},{1,0},{2,3},{3,2},{4,5},{5,4},{6,7},{7,6},{8,9},{9,8},{10,11... | collective-permute-start | bytes 2162696 | tf_op jit(solution)/shard_map/ppermute | solution.py:11
  127.3 18.9 %collective-permute-start.19 = (f32[1472,640]{1,0:T(8,128)S(1)}, f32[1472,640]{1,0:T(8,128)S(1)}, u32[]{:S(2)}, u32[]{:S(2)}) collective-permute-start(f32[1472,640]{1,0:T(8,128)S(1)} %broadcast_select_fusion.2), channel_id=1, source_target_pairs={{0,1},{1,0},{2,3},{3,2},{4,5},{5,4},{6,7},{7,6},{8,9},{9,8},{10,11... | collective-permute-start | bytes 11304968 | tf_op jit(solution)/shard_map/ppermute | solution.py:11
  180.8 10.7 %collective-permute-start.21 = (bf16[96,640]{1,0:T(8,128)(2,1)S(1)}, bf16[96,640]{1,0:T(8,128)(2,1)S(1)}, u32[]{:S(2)}, u32[]{:S(2)}) collective-permute-start(bf16[96,640]{1,0:T(8,128)(2,1)S(1)} %reduce_sum.112), channel_id=1, source_target_pairs={{0,64},{32,96},{64,0},{96,32},{1,65},{33,97},{65,1},{97,33},{2,66}... | collective-permute-start | bytes 368648 | tf_op jit(solution)/shard_map/ppermute | solution.py:11
  180.8 10.7 %collective-permute-start.20 = (bf16[96,640]{1,0:T(8,128)(2,1)S(1)}, bf16[96,640]{1,0:T(8,128)(2,1)S(1)}, u32[]{:S(2)}, u32[]{:S(2)}) collective-permute-start(bf16[96,640]{1,0:T(8,128)(2,1)S(1)} %reduce_sum.112), channel_id=1, source_target_pairs={{0,32},{32,0},{64,96},{96,64},{1,33},{33,1},{65,97},{97,65},{2,34}... | collective-permute-start | bytes 368648 | tf_op jit(solution)/shard_map/ppermute | solution.py:11
  208.9 6.4 %collective-permute-start.31 = (bf16[2,4,24,640]{3,2,1,0:T(8,128)(2,1)S(1)}, bf16[2,4,24,640]{3,2,1,0:T(8,128)(2,1)S(1)}, u32[]{:S(2)}, u32[]{:S(2)}) collective-permute-start(bf16[2,4,24,640]{3,2,1,0:T(8,128)(2,1)S(1)} %pad_maximum_fusion.17), channel_id=1, source_target_pairs={{0,24},{8,16},{16,8},{24,0},{1,25},{9,17},{17,9},{25,1},{2,26},{10... | collective-permute-start | bytes 737288 | tf_op jit(solution)/shard_map/ppermute | solution.py:11
  218.1 11.4 %collective-permute-start.35 = (bf16[1472,640]{1,0:T(8,128)(2,1)S(1)}, bf16[1472,640]{1,0:T(8,128)(2,1)S(1)}, u32[]{:S(2)}, u32[]{:S(2)}) collective-permute-start(bf16[1472,640]{1,0:T(8,128)(2,1)S(1)} %slice.50), channel_id=1, source_target_pairs={{0,1},{1,0},{2,3},{3,2},{4,5},{5,4},{6,7},{7,6},{8,9},{9,8},{10,11... | collective-permute-start | bytes 5652488 | tf_op jit(solution)/shard_map/ppermute | solution.py:11
  (18 other events, 166.8 us)
Sparse Core Ops, SparseCore 0:
  32.0 31.9 all-gather.1

commit v3 on v1

v3 whole, which is shorter than its diff:
```python
import jax
import jax.numpy as jnp
from jax import lax
from jax.sharding import Mesh, PartitionSpec as P

AXES = ("t", "z", "x", "y", "c")
DP = ("z", "x", "y", "c")


def swap(x, axis, mask=1):
    return lax.ppermute(x, axis, [(i, i ^ mask) for i in range(lax.axis_size(axis))])


def row_scales(sums, squares, width):
    average = sums / width
    return average, lax.rsqrt(squares / width - average * average + 1e-06)


def normed(values, average, inverse, gain):
    values = values.astype(jnp.float32)
    return ((values - average) * inverse * gain[None, :]).astype(jnp.bfloat16)


def rounded(x):
    return lax.reduce_precision(x, 8, 7)


def columns_of(vectors, count=128):
    column = lax.broadcasted_iota(jnp.int32, (vectors[0].shape[0], count), 1)
    block = jnp.zeros(column.shape, jnp.float32)
    for i, rest in enumerate(vectors):
        for k in range(3):
            piece = rounded(rest)
            block = jnp.where(column == 3 * i + k, piece[:, None], block)
            rest = rest - piece
    return block.astype(jnp.bfloat16)


def vector_of(block, i):
    return jnp.sum(block[:, 3 * i : 3 * i + 3].astype(jnp.float32), axis=1, keepdims=True)


def packed_rows(projected, average, inverse):
    length = jnp.sqrt(jnp.sum(projected * projected, axis=1, keepdims=True) + 1e-06)
    unit = (projected / length).astype(jnp.bfloat16)
    return jnp.concatenate([unit, columns_of([length[:, 0], average, inverse])], axis=1)


def tied(*arrays):
    return lax.optimization_barrier(arrays)


def gather_text(x):
    halves = jnp.split(x, 2, axis=0)
    orders = ((("x", 1), ("x", 3), ("y", 1)), (("y", 1), ("x", 1), ("x", 3)))
    for step in range(3):
        others = tied(*[swap(h, *order[step]) for h, order in zip(halves, orders)])
        halves = [jnp.concatenate([h, o], axis=0) for h, o in zip(halves, others)]
    return both_cores(jnp.concatenate(halves, axis=0))


def gather_image(x):
    first = swap(x, "y", 3)
    along = jnp.concatenate(tied(*[swap(x, "z", k) for k in (2, 3, 1)]), axis=0)
    return jnp.concatenate([x, along, first, swap(along, "y", 3)], axis=0)


def both_cores(x):
    return jnp.concatenate([x, swap(x, "c")], axis=0)


def by_index(parts, axis):
    index = lax.axis_index(axis)
    even, low = index % 2 == 0, index < 2
    pairs = [
        [jnp.where(even, a, b), jnp.where(even, b, a)] for a, b in (parts[:2], parts[2:])
    ]
    return [jnp.where(low, a, b) for a, b in zip(*pairs)] + [
        jnp.where(low, b, a) for a, b in zip(*pairs)
    ]


def gather_xy(block):
    parts = [part[None, None] for part in jnp.split(block, 2, axis=0)]
    for axes in (("x", "y"), ("y", "x")):
        others = tied(
            *[swap(part, axis, k) for k in (2, 1, 3) for part, axis in zip(parts, axes)]
        )
        parts = [
            jnp.concatenate(
                by_index([part, others[2 + i], others[i], others[4 + i]], axis),
                axis=("x", "y").index(axis),
            )
            for i, (part, axis) in enumerate(zip(parts, axes))
        ]
    parts = [part.reshape((-1,) + part.shape[2:]) for part in parts]
    return jnp.concatenate(parts, axis=1)


def slope(gradient, packed, width):
    unit = packed[:, :width].astype(jnp.float32)
    length = vector_of(packed[:, width:], 0)
    along = jnp.sum(unit * gradient, axis=1, keepdims=True)
    value = (gradient - unit * along) / length
    high = rounded(value)
    return high.astype(jnp.bfloat16), (value - high).astype(jnp.bfloat16)


def over_rows(features, slopes):
    return sum(
        lax.dot_general(
            features, part, (((0,), (0,)), ((), ())), preferred_element_type=jnp.float32
        )
        for part in slopes
    )


def per_device(image_x, text_x, image_gain, text_gain, image_w, text_w, sharpness, offset):
    scale, bias = sharpness[0], offset[0]
    towers = lax.axis_size("t")
    rows, width = image_x.shape[0], image_w.shape[1]
    image_values = image_x.astype(jnp.float32)
    text_values = text_x.astype(jnp.float32)
    text_1, image_y = swap(text_x, "x", 1), swap(image_x, "y", 3)
    image_z = [swap(image_x, "z", k) for k in (2, 3, 1)]
    moments = lax.psum(
        (
            jnp.sum(image_values, axis=1),
            jnp.sum(image_values * image_values, axis=1),
            jnp.sum(text_values, axis=1),
            jnp.sum(text_values * text_values, axis=1),
        ),
        "t",
    )
    moments, text_1, image_y, image_z = tied(moments, text_1, image_y, image_z)
    image_scales = row_scales(moments[0], moments[1], image_x.shape[1] * towers)
    text_scales = row_scales(moments[2], moments[3], text_x.shape[1] * towers)
    image_part = jnp.dot(
        normed(image_x, *[v[:, None] for v in image_scales], image_gain),
        image_w,
        preferred_element_type=jnp.float32,
    )
    text_part = jnp.dot(
        normed(text_x, *[v[:, None] for v in text_scales], text_gain),
        text_w,
        preferred_element_type=jnp.float32,
    )
    text_2, image_z = jnp.concatenate([text_x, text_1], axis=0), jnp.concatenate(image_z, axis=0)
    image_far = swap(image_z, "y", 3)
    image_send, text_send, text_3 = tied(
        image_part, text_part, swap(text_2, "x", 3)
    )
    image_other, text_other = swap(image_send, "t"), swap(text_send, "t")
    text_4 = jnp.concatenate([text_2, text_3], axis=0)
    text_8 = jnp.concatenate([text_4, swap(text_4, "y", 1)], axis=0)
    text_other, image_other, text_8, image_far = tied(text_other, image_other, text_8, image_far)
    text_rows = gather_text(packed_rows(text_send + text_other, *text_scales))
    image_rows = gather_image(
        packed_rows(image_send + image_other, *image_scales)
    )
    image_features = jnp.concatenate([image_x, image_z, image_y, image_far], axis=0)
    chips = text_8.reshape(2, 2, 2, 2, rows // 2, text_x.shape[1])
    text_features = both_cores(
        jnp.concatenate(
            [
                chips[:, :, :, 0].reshape(-1, text_x.shape[1]),
                chips[:, :, :, 1].transpose(1, 2, 0, 3, 4).reshape(-1, text_x.shape[1]),
            ],
            axis=0,
        )
    )
    image_normed_rows, text_normed_rows = (
        normed(features, vector_of(block, 1), vector_of(block, 2), gain)
        for features, block, gain in (
            (image_features, image_rows[:, width:], image_gain),
            (text_features, text_rows[:, width:], text_gain),
        )
    )

    image_units, text_units = image_rows[:, :width], text_rows[:, :width]
    products = lax.dot_general(
        image_units, text_units, (((1,), (1,)), ((), ())), preferred_element_type=jnp.float32
    )
    logits = scale * products + bias
    half = rows // 2
    row_ids = lax.broadcasted_iota(jnp.int32, products.shape, 0)
    column_ids = lax.broadcasted_iota(jnp.int32, products.shape, 1)
    same = ((column_ids == row_ids) & (row_ids < half)) | (
        (column_ids == row_ids + 7 * half) & (row_ids >= half) & (row_ids < rows)
    )
    labels = jnp.where(same, 1.0, -1.0).astype(jnp.float32)
    weights = (-labels * jax.nn.sigmoid(-labels * logits)).astype(jnp.bfloat16)
    image_grad = scale * jnp.dot(weights, text_units, preferred_element_type=jnp.float32)
    text_grad = scale * lax.dot_general(
        weights, image_units, (((0,), (0,)), ((), ())), preferred_element_type=jnp.float32
    )
    image_slope = slope(image_grad, image_rows, width)
    text_slope = slope(text_grad, text_rows, width)
    image_term = over_rows(image_normed_rows, image_slope)
    text_term = over_rows(text_normed_rows, text_slope)
    plane = lax.axis_size("x") * lax.axis_size("y")
    deep, depth = image_w.shape[0] + text_w.shape[0], image_w.shape[0]
    each = -(-deep // (2 * plane * 16)) * 16
    term = jnp.concatenate(
        [image_term, text_term, jnp.zeros((2 * plane * each - deep, width), jnp.float32)], axis=0
    )
    lower, upper = jnp.split(term, 2, axis=0)
    first = lax.axis_index("c") == 0
    kept = jnp.where(first, lower, upper) + swap(jnp.where(first, upper, lower), "c")
    blocks = kept.astype(jnp.bfloat16).reshape(plane, each, width)
    blocks = lax.all_to_all(blocks, ("x", "y"), 0, 0)
    block = rounded(jnp.sum(blocks.astype(jnp.float32), axis=0))
    others = tied(*[swap(block.astype(jnp.bfloat16), "z", k) for k in (2, 3, 1)])
    z2, z3, z1 = [other.astype(jnp.float32) for other in others]
    block = ((block + z1) + (z2 + z3)).astype(jnp.bfloat16)
    block = gather_xy(block).reshape(plane * each, width)
    other = swap(block, "c")
    full = jnp.concatenate(
        [jnp.where(first, block, other), jnp.where(first, other, block)], axis=0
    ).astype(jnp.float32)
    return full[:depth], full[depth:deep]


def solution(mesh):
    grid = Mesh(mesh.devices.reshape(2, 4, 4, 4, 2), AXES)
    return jax.shard_map(
        per_device,
        mesh=grid,
        in_specs=(
            P(DP, "t"),
            P(DP, "t"),
            P("t"),
            P("t"),
            P("t", None),
            P("t", None),
            P(),
            P(),
        ),
        out_specs=(P("t", None), P("t", None)),
        check_vma=False,
    )
```

time: 262 us -> 229 us (0.87); the launches traced: 262 us -> 224 us
  blocking collectives: 106 us -> 37.4 us
  starting transfers between devices: 20.4 us -> 82.8 us
  waiting for transfers between devices: 77.9 us -> 59.4 us
  between operations: 15.3 us -> 2.77 us
  matrix products: 21.2 us -> 26.2 us
  local copies, waits for them, and re-layouts: 8.28 us -> 5.48 us
    all_gather x5 -> x0, blocking collectives: 65.3 us -> none  [the longest x3 34.7 us: gather_xy(): x = lax.all_gather(x, 'y', axis=0, tiled=True)]
    ppermute x9 -> x40, starting transfers between devices: 20.1 us -> 82.8 us  [swap(): lax.ppermute(x, axis, [(i, i ^ mask) for i in range(lax.axis_size(axis))])]
    all_gather x3 -> x0, waiting for transfers between devices: 49.8 us -> none  [gather_xy(): return lax.all_gather(x, 'x', axis=0, tiled=True)]
    ppermute x9 -> x40, waiting for transfers between devices: 28.1 us -> 59.4 us  [swap(): lax.ppermute(x, axis, [(i, i ^ mask) for i in range(lax.axis_size(axis))])]
    dot_general x4 -> x6, matrix products: 11.4 us -> 20.2 us  [the longest x4 17.7 us: over_rows(): lax.dot_general(features, part, (((0,), (0,)), ((), ())), preferred_eleme...]
    reshape x2 -> x0, local copies, waits for them, and re-layouts: 5.93 us -> none  [the longest x1 3.52 us: per_device(): blocks = kept.reshape(groups, kept.shape[0] // groups, half)]
    convert_element_type x3 -> x5, other arithmetic: 3.63 us -> 0.93 us  [the longest x1 0.56 us: per_device(): blocks = kept.astype(jnp.bfloat16).reshape(plane, each, width)]
  transfers between devices with their start and end apart: 12 -> 40, of which waited for: 8 -> 21; matrix products, arithmetic and copies ran while one was open for 6% -> 8% of each run, Pallas kernels for 0% -> 0%
where the time goes in v3:
time: 229 us; the launch traced here: 224 us
  starting transfers between devices  82.8 us (36%)
  waiting for transfers between devices  59.4 us (26%)
  blocking collectives  37.4 us (16%)
  matrix products  26.2 us (11%)
  other arithmetic  10.1 us (4%)
  local copies, waits for them, and re-layouts  5.48 us (2%)
  between operations  2.77 us (1%)
    ppermute x40, starting transfers between devices, swap(): lax.ppermute(x, axis, [(i, i ^ mask) for i in range(lax.axis_size(axis))])  82.8 us
    ppermute x40, waiting for transfers between devices, swap(): lax.ppermute(x, axis, [(i, i ^ mask) for i in range(lax.axis_size(axis))])  59.4 us
    all_to_all x1, blocking collectives, per_device(): blocks = lax.all_to_all(blocks, ('x', 'y'), 0, 0)  29.6 us
    dot_general x4, matrix products, over_rows(): lax.dot_general(features, part, (((0,), (0,)), ((), ())), preferred_eleme...  17.7 us
    psum x1, blocking collectives, per_device(): lax.psum((jnp.sum(image_values, axis=1), jnp.sum(image_values * image_val...  7.77 us
  transfers between devices with their start and end apart: 40, of which 21 were waited for; matrix products, arithmetic and copies ran while one was open for 8% of the time, Pallas kernels for 0%

profile of v3, /device:TPU:1, one launch (start us, length us, event | category | flops | bytes accessed | tf_op | source)
XLA Modules:
  0.0 224.1 jit_solution(1041239706878783332)
XLA Ops:
  0.7 3.7 %collective-permute-start.1 = (bf16[64,832]{1,0:T(8,128)(2,1)}, bf16[64,832]{1,0:T(8,128)(2,1)S(1)}, u32[]{:S(2)}, u32[]{:S(2)}) collective-permute-start(bf16[64,832]{1,0:T(8,128)(2,1)} %param.8), channel_id=1, source_target_pairs={{0,6},{2,4},{4,2},{6,0},{1,7},{3,5},{5,3},{7,1},{8,14},{10,12},{12... | collective-permute-start | bytes 319496 | tf_op jit(solution)/shard_map/ppermute | solution.py:11
  4.3 3.0 %collective-permute-start.2 = (bf16[64,832]{1,0:T(8,128)(2,1)}, bf16[64,832]{1,0:T(8,128)(2,1)S(1)}, u32[]{:S(2)}, u32[]{:S(2)}) collective-permute-start(bf16[64,832]{1,0:T(8,128)(2,1)} %param.8), channel_id=1, source_target_pairs={{0,64},{32,96},{64,0},{96,32},{1,65},{33,97},{65,1},{97,33},{2,66}... | collective-permute-start | bytes 319496 | tf_op jit(solution)/shard_map/ppermute | solution.py:11
  15.2 7.8 %all-reduce = (f32[64]{0:T(128)S(1)}, f32[64]{0:T(128)S(1)}, f32[64]{0:T(128)S(1)}, f32[64]{0:T(128)S(1)}) all-reduce(f32[64]{0:T(128)S(1)} %get-tuple-element.89, f32[64]{0:T(128)S(1)} %get-tuple-element.88, f32[64]{0:T(128)S(1)} %get-tuple-element.91, f32[64]{0:T(128)S(1)} %get-tuple-element.90), channel_id=1, replica_groups=mesh['t'=2,'z'=4,'x'=4,'y'=4,'c'=2] {'t'}, use_global_device_ids=true, to_apply=%region_1.0 | all-reduce | flops 256 | bytes 2048 | tf_op jit(solution)/shard_map/psum | solution.py:126
  29.6 5.1 %collective-permute-start.6 = (f32[64,1280]{1,0:T(8,128)S(1)}, f32[64,1280]{1,0:T(8,128)S(1)}, u32[]{:S(2)}, u32[]{:S(2)}) collective-permute-start(f32[64,1280]{1,0:T(8,128)S(1)} %fusion.39), channel_id=1, source_target_pairs={{0,128},{128,0},{1,129},{129,1},{2,130},{130,2},{3,131},{131,3},{4... | collective-permute-start | bytes 983048 | tf_op jit(solution)/shard_map/ppermute | solution.py:11
  35.9 3.8 %collective-permute-done.6 = f32[64,1280]{1,0:T(8,128)S(1)} collective-permute-done((f32[64,1280]{1,0:T(8,128)S(1)}, f32[64,1280]{1,0:T(8,128)S(1)}, u32[]{:S(2)}, u32[]{:S(2)}) %collective-permute-start.6) | collective-permute-done | bytes 327712 | tf_op jit(solution)/shard_map/ppermute | solution.py:11
  39.6 10.3 %collective-permute-done.7 = f32[64,1280]{1,0:T(8,128)S(1)} collective-permute-done((f32[64,1280]{1,0:T(8,128)S(1)}, f32[64,1280]{1,0:T(8,128)S(1)}, u32[]{:S(2)}, u32[]{:S(2)}) %collective-permute-start.7) | collective-permute-done | bytes 327712 | tf_op jit(solution)/shard_map/ppermute | solution.py:11
  50.6 14.8 %collective-permute-start.10 = (bf16[64,1408]{1,0:T(8,128)(2,1)S(1)}, bf16[64,1408]{1,0:T(8,128)(2,1)S(1)}, u32[]{:S(2)}, u32[]{:S(2)}) collective-permute-start(bf16[64,1408]{1,0:T(8,128)(2,1)S(1)} %get-tuple-element.133), channel_id=1, source_target_pairs={{0,64},{32,96},{64,0},{96,32},{1,65},{33,97},{65,1},{97,33},{2,66}... | collective-permute-start | bytes 540680 | tf_op jit(solution)/shard_map/ppermute | solution.py:11
  75.9 2.6 %collective-permute-done.17 = bf16[64,1408]{1,0:T(8,128)(2,1)S(1)} collective-permute-done((bf16[64,1408]{1,0:T(8,128)(2,1)S(1)}, bf16[64,1408]{1,0:T(8,128)(2,1)S(1)}, u32[]{:S(2)}, u32[]{:S(2)}) %collective-permute-start.17) | collective-permute-done | bytes 180256 | tf_op jit(solution)/shard_map/ppermute | solution.py:11
  78.5 2.0 collective-permute-start.20
  83.9 5.8 %collective-permute-start.22 = (bf16[512,640]{1,0:T(8,128)(2,1)S(1)}, bf16[512,640]{1,0:T(8,128)(2,1)S(1)}, u32[]{:S(2)}, u32[]{:S(2)}) collective-permute-start(bf16[512,640]{1,0:T(8,128)(2,1)S(1)} %pad_maximum_fusion.5), channel_id=1, source_target_pairs={{0,1},{1,0},{2,3},{3,2},{4,5},{5,4},{6,7},{7,6},{8,9},{9,8},{10,11... | collective-permute-start | bytes 1966088 | tf_op jit(solution)/shard_map/ppermute | solution.py:11
  89.9 3.8 %collective-permute-start.21 = (bf16[512,1408]{1,0:T(8,128)(2,1)S(1)}, bf16[512,1408]{1,0:T(8,128)(2,1)S(1)}, u32[]{:S(2)}, u32[]{:S(2)}) collective-permute-start(bf16[512,1408]{1,0:T(8,128)(2,1)S(1)} %get-tuple-element.116), channel_id=1, source_target_pairs={{0,1},{1,0},{2,3},{3,2},{4,5},{5,4},{6,7},{7,6},{8,9},{9,8},{10,11... | collective-permute-start | bytes 4325384 | tf_op jit(solution)/shard_map/ppermute | solution.py:11
  95.5 13.4 %collective-permute-done.14 = bf16[192,1408]{1,0:T(8,128)(2,1)S(1)} collective-permute-done((bf16[192,1408]{1,0:T(8,128)(2,1)S(1)}, bf16[192,1408]{1,0:T(8,128)(2,1)S(1)}, u32[]{:S(2)}, u32[]{:S(2)}) %collective-permute-start.14) | collective-permute-done | bytes 540704 | tf_op jit(solution)/shard_map/ppermute | solution.py:11
  109.5 2.3 %multiply_convert_fusion.1 = bf16[512,1024]{1,0:T(8,128)(2,1)S(1)} fusion(bf16[1024,1408]{1,0:T(8,128)(2,1)S(1)} %constant_dynamic-update-slice_fusion.20, f32[]{:T(128)} %bitcast.44, f32[]{:T(128)} %bitcast.40, s32[512]{0:T(512)S(1)} %iota_add_fusion, pred[512]{0:T(512)(128)(4,1)S(1)} %get-tuple-element.182, pred[512]{0:T(512)(128)(4,1)S(1)} %get-tuple-element.183, ...), kind=kOutput, calls=%fused_computation.29 | convolution fusion | flops 1350565888 | bytes 4984328 | tf_op jit(solution)/shard_map/dot_general | solution.py:181
  117.4 2.0 fusion
  119.4 2.7 %fusion.9 = f32[640,1280]{1,0:T(8,128)S(1)} fusion(bf16[512,640]{1,0:T(8,128)(2,1)S(1)} %collective-permute-done.22, bf16[256,640]{1,0:T(8,128)(2,1)S(1)} %bitcast.54, bf16[256,640]{1,0:T(8,128)(2,1)S(1)} %bitcast.51, f32[640]{0:T(1024)S(1)} %copy-done.6, f32[1024]{0:T(1024)S(1)} %get-tuple-element.83, f32[1024]{0:T(1024)S(1)} %get-tuple-element.84, ...), kind=kOutput, calls=%fused_computation.27 | convolution fusion | flops 1694760960 | bytes 12472324 | tf_op jit(solution)/shard_map/dot_general | solution.py:111
  122.1 11.6 %convolution_add_fusion.1 = f32[640,1280]{1,0:T(8,128)S(1)} fusion(f32[640,1280]{1,0:T(8,128)S(1)} %fusion.9, bf16[512,640]{1,0:T(8,128)(2,1)S(1)} %collective-permute-done.22, bf16[256,640]{1,0:T(8,128)(2,1)S(1)} %bitcast.55, bf16[256,640]{1,0:T(8,128)(2,1)S(1)} %bitcast.52, f32[640]{0:T(1024)S(1)} %copy-done.6, f32[1024]{0:T(1024)S(1)} %get-tuple-element.83, ...), kind=kOutput, calls=%fused_computation.17 | convolution fusion | flops 1694269440 | bytes 15749124 | tf_op jit(solution)/shard_map/dot_general | solution.py:111
  135.1 6.4 %collective-permute-done.23 = f32[768,1280]{1,0:T(8,128)S(1)} collective-permute-done((f32[768,1280]{1,0:T(8,128)S(1)}, f32[768,1280]{1,0:T(8,128)S(1)}, u32[]{:S(2)}, u32[]{:S(2)}) %collective-permute-start.23) | collective-permute-done | bytes 3932192 | tf_op jit(solution)/shard_map/ppermute | solution.py:11
  142.1 29.6 %all_to_all.5 = bf16[16,48,1280]{2,1,0:T(8,128)(2,1)S(1)} all-to-all(bf16[16,48,1280]{2,1,0:T(8,128)(2,1)S(1)} %bitcast.46), channel_id=1, replica_groups=mesh['t'=2,'z'=4,'x'=4,'y'=4,'c'=2] {'x','y'}, dimensions={0} | all-to-all | bytes 3932160 | tf_op jit(solution)/shard_map/all_to_all | solution.py:211
  172.0 2.4 %collective-permute-start.24 = (bf16[48,1280]{1,0:T(8,128)(2,1)S(1)}, bf16[48,1280]{1,0:T(8,128)(2,1)S(1)}, u32[]{:S(2)}, u32[]{:S(2)}) collective-permute-start(bf16[48,1280]{1,0:T(8,128)(2,1)S(1)} %reduce-precision_convert_fusion.4), channel_id=1, source_target_pairs={{0,64},{32,96},{64,0},{96,32},{1,65},{33,97},{65,1},{97,33},{2,66}... | collective-permute-start | bytes 368648 | tf_op jit(solution)/shard_map/ppermute | solution.py:11
  176.7 3.4 %collective-permute-done.25 = bf16[48,1280]{1,0:T(8,128)(2,1)S(1)} collective-permute-done((bf16[48,1280]{1,0:T(8,128)(2,1)S(1)}, bf16[48,1280]{1,0:T(8,128)(2,1)S(1)}, u32[]{:S(2)}, u32[]{:S(2)}) %collective-permute-start.25) | collective-permute-done | bytes 122912 | tf_op jit(solution)/shard_map/ppermute | solution.py:11
  189.7 2.0 collective-permute-done.32
  206.1 8.9 %collective-permute-start.39 = (bf16[768,1280]{1,0:T(8,128)(2,1)S(1)}, bf16[768,1280]{1,0:T(8,128)(2,1)S(1)}, u32[]{:S(2)}, u32[]{:S(2)}) collective-permute-start(bf16[768,1280]{1,0:T(8,128)(2,1)S(1)} %bitcast.45), channel_id=1, source_target_pairs={{0,1},{1,0},{2,3},{3,2},{4,5},{5,4},{6,7},{7,6},{8,9},{9,8},{10,11... | collective-permute-start | bytes 5898248 | tf_op jit(solution)/shard_map/ppermute | solution.py:11
  215.0 3.6 %collective-permute-done.39 = bf16[768,1280]{1,0:T(8,128)(2,1)S(1)} collective-permute-done((bf16[768,1280]{1,0:T(8,128)(2,1)S(1)}, bf16[768,1280]{1,0:T(8,128)(2,1)S(1)}, u32[]{:S(2)}, u32[]{:S(2)}) %collective-permute-start.39) | collective-permute-done | bytes 1966112 | tf_op jit(solution)/shard_map/ppermute | solution.py:11
  221.5 2.3 %slice.71 = f32[832,1280]{1,0:T(8,128)} slice(f32[1536,1280]{1,0:T(8,128)S(1)} %maximum_convert_fusion), slice={[0:832], [0:1280]} | slice | bytes 8519680 | tf_op jit(solution)/shard_map/slice | solution.py:221
  (163 shorter events, 68.0 us)
Async XLA Ops:
  0.7 22.4 %collective-permute-start.1 = (bf16[64,832]{1,0:T(8,128)(2,1)}, bf16[64,832]{1,0:T(8,128)(2,1)S(1)}, u32[]{:S(2)}, u32[]{:S(2)}) collective-permute-start(bf16[64,832]{1,0:T(8,128)(2,1)} %param.8), channel_id=1, source_target_pairs={{0,6},{2,4},{4,2},{6,0},{1,7},{3,5},{5,3},{7,1},{8,14},{10,12},{12... | collective-permute-start | bytes 319496 | tf_op jit(solution)/shard_map/ppermute | solution.py:11
  4.3 18.7 %collective-permute-start.2 = (bf16[64,832]{1,0:T(8,128)(2,1)}, bf16[64,832]{1,0:T(8,128)(2,1)S(1)}, u32[]{:S(2)}, u32[]{:S(2)}) collective-permute-start(bf16[64,832]{1,0:T(8,128)(2,1)} %param.8), channel_id=1, source_target_pairs={{0,64},{32,96},{64,0},{96,32},{1,65},{33,97},{65,1},{97,33},{2,66}... | collective-permute-start | bytes 319496 | tf_op jit(solution)/shard_map/ppermute | solution.py:11
  7.3 15.7 %collective-permute-start.3 = (bf16[64,832]{1,0:T(8,128)(2,1)}, bf16[64,832]{1,0:T(8,128)(2,1)S(1)}, u32[]{:S(2)}, u32[]{:S(2)}) collective-permute-start(bf16[64,832]{1,0:T(8,128)(2,1)} %param.8), channel_id=1, source_target_pairs={{0,96},{32,64},{64,32},{96,0},{1,97},{33,65},{65,33},{97,1},{2,98}... | collective-permute-start | bytes 319496 | tf_op jit(solution)/shard_map/ppermute | solution.py:11
  8.7 14.4 %collective-permute-start.4 = (bf16[64,832]{1,0:T(8,128)(2,1)}, bf16[64,832]{1,0:T(8,128)(2,1)S(1)}, u32[]{:S(2)}, u32[]{:S(2)}) collective-permute-start(bf16[64,832]{1,0:T(8,128)(2,1)} %param.8), channel_id=1, source_target_pairs={{0,32},{32,0},{64,96},{96,64},{1,33},{33,1},{65,97},{97,65},{2,34}... | collective-permute-start | bytes 319496 | tf_op jit(solution)/shard_map/ppermute | solution.py:11
  9.0 14.1 %collective-permute-start = (bf16[64,640]{1,0:T(8,128)(2,1)}, bf16[64,640]{1,0:T(8,128)(2,1)S(1)}, u32[]{:S(2)}, u32[]{:S(2)}) collective-permute-start(bf16[64,640]{1,0:T(8,128)(2,1)} %param.9), channel_id=1, source_target_pairs={{0,8},{8,0},{16,24},{24,16},{1,9},{9,1},{17,25},{25,17},{2,10},{10... | collective-permute-start | bytes 245768 | tf_op jit(solution)/shard_map/ppermute | solution.py:11
  25.9 9.9 %collective-permute-start.9 = (bf16[192,832]{1,0:T(8,128)(2,1)S(1)}, bf16[192,832]{1,0:T(8,128)(2,1)S(1)}, u32[]{:S(2)}, u32[]{:S(2)}) collective-permute-start(bf16[192,832]{1,0:T(8,128)(2,1)S(1)} %pad_maximum_fusion.9), channel_id=1, source_target_pairs={{0,6},{2,4},{4,2},{6,0},{1,7},{3,5},{5,3},{7,1},{8,14},{10,12},{12... | collective-permute-start | bytes 958472 | tf_op jit(solution)/shard_map/ppermute | solution.py:11
  29.6 10.0 %collective-permute-start.6 = (f32[64,1280]{1,0:T(8,128)S(1)}, f32[64,1280]{1,0:T(8,128)S(1)}, u32[]{:S(2)}, u32[]{:S(2)}) collective-permute-start(f32[64,1280]{1,0:T(8,128)S(1)} %fusion.39), channel_id=1, source_target_pairs={{0,128},{128,0},{1,129},{129,1},{2,130},{130,2},{3,131},{131,3},{4... | collective-permute-start | bytes 983048 | tf_op jit(solution)/shard_map/ppermute | solution.py:11
  34.7 15.2 %collective-permute-start.7 = (f32[64,1280]{1,0:T(8,128)S(1)}, f32[64,1280]{1,0:T(8,128)S(1)}, u32[]{:S(2)}, u32[]{:S(2)}) collective-permute-start(f32[64,1280]{1,0:T(8,128)S(1)} %fusion.33), channel_id=1, source_target_pairs={{0,128},{128,0},{1,129},{129,1},{2,130},{130,2},{3,131},{131,3},{4... | collective-permute-start | bytes 983048 | tf_op jit(solution)/shard_map/ppermute | solution.py:11
  50.6 31.5 %collective-permute-start.10 = (bf16[64,1408]{1,0:T(8,128)(2,1)S(1)}, bf16[64,1408]{1,0:T(8,128)(2,1)S(1)}, u32[]{:S(2)}, u32[]{:S(2)}) collective-permute-start(bf16[64,1408]{1,0:T(8,128)(2,1)S(1)} %get-tuple-element.133), channel_id=1, source_target_pairs={{0,64},{32,96},{64,0},{96,32},{1,65},{33,97},{65,1},{97,33},{2,66}... | collective-permute-start | bytes 540680 | tf_op jit(solution)/shard_map/ppermute | solution.py:11
  65.4 18.4 %collective-permute-start.11 = (bf16[64,1408]{1,0:T(8,128)(2,1)S(1)}, bf16[64,1408]{1,0:T(8,128)(2,1)S(1)}, u32[]{:S(2)}, u32[]{:S(2)}) collective-permute-start(bf16[64,1408]{1,0:T(8,128)(2,1)S(1)} %get-tuple-element.133), channel_id=1, source_target_pairs={{0,96},{32,64},{64,32},{96,0},{1,97},{33,65},{65,33},{97,1},{2,98}... | collective-permute-start | bytes 540680 | tf_op jit(solution)/shard_map/ppermute | solution.py:11
  67.1 22.5 %collective-permute-start.12 = (bf16[64,1408]{1,0:T(8,128)(2,1)S(1)}, bf16[64,1408]{1,0:T(8,128)(2,1)S(1)}, u32[]{:S(2)}, u32[]{:S(2)}) collective-permute-start(bf16[64,1408]{1,0:T(8,128)(2,1)S(1)} %get-tuple-element.133), channel_id=1, source_target_pairs={{0,32},{32,0},{64,96},{96,64},{1,33},{33,1},{65,97},{97,65},{2,34}... | collective-permute-start | bytes 540680 | tf_op jit(solution)/shard_map/ppermute | solution.py:11
  78.5 11.1 %collective-permute-start.20 = (bf16[128,1408]{1,0:T(8,128)(2,1)S(1)}, bf16[128,1408]{1,0:T(8,128)(2,1)S(1)}, u32[]{:S(2)}, u32[]{:S(2)}) collective-permute-start(bf16[128,1408]{1,0:T(8,128)(2,1)S(1)} %pad_maximum_fusion.8), channel_id=1, source_target_pairs={{0,24},{8,16},{16,8},{24,0},{1,25},{9,17},{17,9},{25,1},{2,26},{10... | collective-permute-start | bytes 1081352 | tf_op jit(solution)/shard_map/ppermute | solution.py:11
  80.5 9.1 %collective-permute-start.19 = (bf16[128,1408]{1,0:T(8,128)(2,1)S(1)}, bf16[128,1408]{1,0:T(8,128)(2,1)S(1)}, u32[]{:S(2)}, u32[]{:S(2)}) collective-permute-start(bf16[128,1408]{1,0:T(8,128)(2,1)S(1)} %pad_maximum_fusion.7), channel_id=1, source_target_pairs={{0,2},{2,0},{4,6},{6,4},{1,3},{3,1},{5,7},{7,5},{8,10},{10,8},{12,... | collective-permute-start | bytes 1081352 | tf_op jit(solution)/shard_map/ppermute | solution.py:11
  82.1 13.4 %collective-permute-start.13 = (bf16[64,1408]{1,0:T(8,128)(2,1)S(1)}, bf16[64,1408]{1,0:T(8,128)(2,1)S(1)}, u32[]{:S(2)}, u32[]{:S(2)}) collective-permute-start(bf16[64,1408]{1,0:T(8,128)(2,1)S(1)} %get-tuple-element.133), channel_id=1, source_target_pairs={{0,6},{2,4},{4,2},{6,0},{1,7},{3,5},{5,3},{7,1},{8,14},{10,12},{12... | collective-permute-start | bytes 540680 | tf_op jit(solution)/shard_map/ppermute | solution.py:11
  83.9 35.6 %collective-permute-start.22 = (bf16[512,640]{1,0:T(8,128)(2,1)S(1)}, bf16[512,640]{1,0:T(8,128)(2,1)S(1)}, u32[]{:S(2)}, u32[]{:S(2)}) collective-permute-start(bf16[512,640]{1,0:T(8,128)(2,1)S(1)} %pad_maximum_fusion.5), channel_id=1, source_target_pairs={{0,1},{1,0},{2,3},{3,2},{4,5},{5,4},{6,7},{7,6},{8,9},{9,8},{10,11... | collective-permute-start | bytes 1966088 | tf_op jit(solution)/shard_map/ppermute | solution.py:11
  89.9 19.4 %collective-permute-start.21 = (bf16[512,1408]{1,0:T(8,128)(2,1)S(1)}, bf16[512,1408]{1,0:T(8,128)(2,1)S(1)}, u32[]{:S(2)}, u32[]{:S(2)}) collective-permute-start(bf16[512,1408]{1,0:T(8,128)(2,1)S(1)} %get-tuple-element.116), channel_id=1, source_target_pairs={{0,1},{1,0},{2,3},{3,2},{4,5},{5,4},{6,7},{7,6},{8,9},{9,8},{10,11... | collective-permute-start | bytes 4325384 | tf_op jit(solution)/shard_map/ppermute | solution.py:11
  93.8 15.2 %collective-permute-start.14 = (bf16[192,1408]{1,0:T(8,128)(2,1)S(1)}, bf16[192,1408]{1,0:T(8,128)(2,1)S(1)}, u32[]{:S(2)}, u32[]{:S(2)}) collective-permute-start(bf16[192,1408]{1,0:T(8,128)(2,1)S(1)} %pad_maximum_fusion.6), channel_id=1, source_target_pairs={{0,6},{2,4},{4,2},{6,0},{1,7},{3,5},{5,3},{7,1},{8,14},{10,12},{12... | collective-permute-start | bytes 1622024 | tf_op jit(solution)/shard_map/ppermute | solution.py:11
  134.2 7.3 %collective-permute-start.23 = (f32[768,1280]{1,0:T(8,128)S(1)}, f32[768,1280]{1,0:T(8,128)S(1)}, u32[]{:S(2)}, u32[]{:S(2)}) collective-permute-start(f32[768,1280]{1,0:T(8,128)S(1)} %slice_select_fusion), channel_id=1, source_target_pairs={{0,1},{1,0},{2,3},{3,2},{4,5},{5,4},{6,7},{7,6},{8,9},{9,8},{10,11... | collective-permute-start | bytes 11796488 | tf_op jit(solution)/shard_map/ppermute | solution.py:11
  191.8 6.7 %collective-permute-start.34 = (bf16[1,4,24,1280]{3,2,1,0:T(8,128)(2,1)S(1)}, bf16[1,4,24,1280]{3,2,1,0:T(8,128)(2,1)S(1)}, u32[]{:S(2)}, u32[]{:S(2)}) collective-permute-start(bf16[1,4,24,1280]{3,2,1,0:T(8,128)(2,1)S(1)} %pad_maximum_fusion.12), channel_id=1, source_target_pairs={{0,16},{8,24},{16,0},{24,8},{1,17},{9,25},{17,1},{25,9},{2,18},{10... | collective-permute-start | bytes 737288 | tf_op jit(solution)/shard_map/ppermute | solution.py:11
  193.3 6.8 %collective-permute-start.36 = (bf16[1,4,24,1280]{3,2,1,0:T(8,128)(2,1)S(1)}, bf16[1,4,24,1280]{3,2,1,0:T(8,128)(2,1)S(1)}, u32[]{:S(2)}, u32[]{:S(2)}) collective-permute-start(bf16[1,4,24,1280]{3,2,1,0:T(8,128)(2,1)S(1)} %pad_maximum_fusion.12), channel_id=1, source_target_pairs={{0,8},{8,0},{16,24},{24,16},{1,9},{9,1},{17,25},{25,17},{2,10},{10... | collective-permute-start | bytes 737288 | tf_op jit(solution)/shard_map/ppermute | solution.py:11
  193.5 7.6 %collective-permute-start.38 = (bf16[1,4,24,1280]{3,2,1,0:T(8,128)(2,1)S(1)}, bf16[1,4,24,1280]{3,2,1,0:T(8,128)(2,1)S(1)}, u32[]{:S(2)}, u32[]{:S(2)}) collective-permute-start(bf16[1,4,24,1280]{3,2,1,0:T(8,128)(2,1)S(1)} %pad_maximum_fusion.12), channel_id=1, source_target_pairs={{0,24},{8,16},{16,8},{24,0},{1,25},{9,17},{17,9},{25,1},{2,26},{10... | collective-permute-start | bytes 737288 | tf_op jit(solution)/shard_map/ppermute | solution.py:11
  196.8 6.9 %collective-permute-start.35 = (bf16[4,1,24,1280]{3,2,1,0:T(8,128)(2,1)S(1)}, bf16[4,1,24,1280]{3,2,1,0:T(8,128)(2,1)S(1)}, u32[]{:S(2)}, u32[]{:S(2)}) collective-permute-start(bf16[4,1,24,1280]{3,2,1,0:T(8,128)(2,1)S(1)} %pad_maximum_fusion.11), channel_id=1, source_target_pairs={{0,2},{2,0},{4,6},{6,4},{1,3},{3,1},{5,7},{7,5},{8,10},{10,8},{12,... | collective-permute-start | bytes 737288 | tf_op jit(solution)/shard_map/ppermute | solution.py:11
  198.6 6.7 %collective-permute-start.37 = (bf16[4,1,24,1280]{3,2,1,0:T(8,128)(2,1)S(1)}, bf16[4,1,24,1280]{3,2,1,0:T(8,128)(2,1)S(1)}, u32[]{:S(2)}, u32[]{:S(2)}) collective-permute-start(bf16[4,1,24,1280]{3,2,1,0:T(8,128)(2,1)S(1)} %pad_maximum_fusion.11), channel_id=1, source_target_pairs={{0,6},{2,4},{4,2},{6,0},{1,7},{3,5},{5,3},{7,1},{8,14},{10,12},{12... | collective-permute-start | bytes 737288 | tf_op jit(solution)/shard_map/ppermute | solution.py:11
  206.1 12.5 %collective-permute-start.39 = (bf16[768,1280]{1,0:T(8,128)(2,1)S(1)}, bf16[768,1280]{1,0:T(8,128)(2,1)S(1)}, u32[]{:S(2)}, u32[]{:S(2)}) collective-permute-start(bf16[768,1280]{1,0:T(8,128)(2,1)S(1)} %bitcast.45), channel_id=1, source_target_pairs={{0,1},{1,0},{2,3},{3,2},{4,5},{5,4},{6,7},{7,6},{8,9},{9,8},{10,11... | collective-permute-start | bytes 5898248 | tf_op jit(solution)/shard_map/ppermute | solution.py:11
  (23 other events, 173.6 us)
